TPU v7x, 128 devices: a whole 4x4x4 slice. The times are simulated.
128 devices in a mesh: section: 2 (over y_hi), shard: 16 (over y_lo, z, core), rep: 4 (over x).
Axes of the slice: x: 4, y: 4 (y_hi: 2, y_lo: 2; y = y_hi * 2 + y_lo), z: 4, core: 2. Of those that a mesh axis runs over, the one named last changes fastest.
Arguments:
- tokens: bfloat16 [2, 7168, 1024], P(None, ('shard', 'rep')), may hold values from -6 to 6
- segment_ids: int32 [2, 64, 112], P(None, ('shard', 'rep')), may hold values from 0 to 3, never falling along the last dimension, each value on 1 to 56 neighbouring positions
- cotangent: bfloat16 [2, 7168, 1024], P(None, ('shard', 'rep')), may hold values from -6 to 6
- norm_gains: bfloat16 [2, 1024, 2], P('section', 'shard'), may hold values from 0.5 to 1.5
- w_in: bfloat16 [2, 1024, 4120], P('section', 'shard'), may hold values from -0.1875 to 0.1875
- conv_params: bfloat16 [2, 1792, 5], P('section', 'shard'), may hold values from -1.5 to 1.5
- head_params: bfloat16 [2, 24, 3], P('section'), may hold values from -6.9 to 2.77, as said below
- w_out: bfloat16 [2, 2048, 1024], P('section', 'shard'), may hold values from -0.25 to 0.25
- w_gate_up: bfloat16 [2, 1024, 4096], P('section', 'shard'), may hold values from -0.1875 to 0.1875
- w_down: bfloat16 [2, 2048, 1024], P('section', 'shard'), may hold values from -0.125 to 0.125
Outputs:
- layer_out: bfloat16 [2, 2, 7168, 1024], P('section', None, ('shard', 'rep'))
- input_grads: float32 [2, 2, 7168, 1024], P('section', None, ('shard', 'rep'))
- grad_gains: float32 [2, 1024, 2], P('section', 'shard')
- grad_w_in: float32 [2, 1024, 4120], P('section', 'shard')
- grad_conv: float32 [2, 1792, 5], P('section', 'shard')
- grad_heads: float32 [2, 24, 3], P('section')
- grad_w_out: float32 [2, 2048, 1024], P('section', 'shard')
- grad_gate_up: float32 [2, 1024, 4096], P('section', 'shard')
- grad_w_down: float32 [2, 2048, 1024], P('section', 'shard')
Inputs may be any that keep to these rules, and one draw needn't show every extreme that they name: `segment_ids`: in each block of 112 slots the numbers never fall; each sequence holds 1 to 56 slots, and one holds exactly 56. `head_params`: column 0 (step bias) lies in -6.9 to -2.3, column 1 (log of the decay rate) in 0 to 2.77, column 2 (skip factor) in -1 to 1.
All inputs are finite; a program needn't handle non-finite values.
Results may differ from a plain program's by a relative error of at most 0.024.
Values may be sent and summed in bfloat16 or wider, within the bound.
A program may use at most 256 MiB of HBM per device.

v0:
```python
import itertools
import math

import jax
import jax.numpy as jnp
from jax import lax
from jax.experimental import pallas as pl
from jax.experimental.pallas import tpu as pltpu
from jax.sharding import PartitionSpec as P

FF = 2048
MHEADS = 24
HEAD_WIDTH = 64
STATE = 128
QUERY_HEAD_COUNT = 8
KVHEADS = 2
CONV = 4
SSM = 1536
CH = 1792
UW = 2048
PIN = 4120
PAD = 4224
T = 112
OFF_Q = SSM + CH
OFF_K = OFF_Q + QUERY_HEAD_COUNT * HEAD_WIDTH
OFF_V = OFF_K + KVHEADS * HEAD_WIDTH
OFF_R = OFF_V + KVHEADS * HEAD_WIDTH
F32 = jnp.float32
BF16 = jnp.bfloat16


def dot_nn(left, right):
    return jnp.dot(left.astype(BF16), right.astype(BF16), preferred_element_type=F32)


def dot_nt(left, right):
    return lax.dot_general(
        left.astype(BF16), right.astype(BF16), (((1,), (1,)), ((), ())), preferred_element_type=F32
    )


def dot_tn(left, right):
    return lax.dot_general(
        left.astype(BF16), right.astype(BF16), (((0,), (0,)), ((), ())), preferred_element_type=F32
    )


def exact_dot(left, right):
    return jnp.dot(left, right, precision=lax.Precision.HIGHEST, preferred_element_type=F32)


def iota(shape, dim):
    return lax.broadcasted_iota(jnp.int32, shape, dim)


def block_masks(segc, segr):
    rows, cols = iota((T, T), 0), iota((T, T), 1)
    allowed = (segc[:, :T] == segr[0:1, :]) & (rows >= cols)
    places = iota((T, 128), 0)
    links = [
        jnp.where((pltpu.roll(segc, j, 0) == segc) & (places >= j), 1.0, 0.0)
        for j in range(1, CONV)
    ]
    return allowed, links


def convolve(p_ref, conv_ref, links, mixed_ref, act_ref):
    for at in range(0, CH, 128):
        sl = slice(at, at + 128)
        c = p_ref[0, :, SSM + at : SSM + at + 128]
        mixed = conv_ref[4:5, sl] + c * conv_ref[0:1, sl]
        for j in range(1, CONV):
            mixed = mixed + links[j - 1] * pltpu.roll(c, j, 0) * conv_ref[j : j + 1, sl]
        if mixed_ref is not None:
            mixed_ref[:, sl] = mixed
        act_ref[:, sl] = mixed * jax.nn.sigmoid(mixed)


def softplus(v):
    return jnp.maximum(v, 0.0) + jnp.log1p(jnp.exp(-jnp.abs(v)))


def steps_and_sums(p_ref, head_ref):
    raw = p_ref[0, :, OFF_R:PAD] + head_ref[0:1, :]
    live = iota((T, 128), 1) < MHEADS
    raw = jnp.where(live, raw, 0.0)
    dt = softplus(raw)
    decay = -dt * jnp.exp(head_ref[1:2, :])
    lower = jnp.where(iota((T, T), 0) >= iota((T, T), 1), 1.0, 0.0)
    return raw, dt, decay, exact_dot(lower, decay)


def attention_probs(q_tile, keep, k_dup, allowed):
    scores = dot_nt(jnp.where(keep, q_tile, 0.0), k_dup) * (1.0 / math.sqrt(HEAD_WIDTH))
    scores = jnp.where(allowed, scores, -1e30)
    e = jnp.exp(scores - jnp.max(scores, -1, keepdims=True))
    return e / jnp.sum(e, -1, keepdims=True)


def doubled(tile, left):
    turned = pltpu.roll(tile, HEAD_WIDTH, 1)
    return jnp.where(left, tile, turned), jnp.where(left, turned, tile)


def mix_forward_kernel(p_ref, segc_ref, segr_ref, conv_ref, head_ref, skip_ref, u_ref, act_ref):
    allowed, links = block_masks(segc_ref[0], segr_ref[0])
    convolve(p_ref, conv_ref, links, None, act_ref)
    _, dt, _, cum = steps_and_sums(p_ref, head_ref)
    dt_t, cum_t = dt.T, cum.T
    left = iota((T, 128), 1) < HEAD_WIDTH
    cb = dot_nt(act_ref[:, SSM + STATE :], act_ref[:, SSM : SSM + STATE])
    for pair in range(MHEADS // 2):
        sl = slice(128 * pair, 128 * pair + 128)
        xs = act_ref[:, sl]
        ys = []
        for h in (2 * pair, 2 * pair + 1):
            decayed = jnp.exp(jnp.where(allowed, cum[:, h : h + 1] - cum_t[h : h + 1, :], -1e30))
            ys.append(dot_nn(decayed * cb * dt_t[h : h + 1, :], xs))
        y = jnp.where(left, ys[0], ys[1]) + skip_ref[0:1, sl] * xs
        z = p_ref[0, :, sl]
        u_ref[0, :, sl] = (y * (z * jax.nn.sigmoid(z))).astype(BF16)
    k_dups = doubled(p_ref[0, :, OFF_K:OFF_V], left)
    v_dups = doubled(p_ref[0, :, OFF_V:OFF_R], left)
    for pair in range(QUERY_HEAD_COUNT // 2):
        kv = pair // 2
        q_tile = p_ref[0, :, OFF_Q + 128 * pair : OFF_Q + 128 * pair + 128]
        probs = [attention_probs(q_tile, keep, k_dups[kv], allowed) for keep in (left, ~left)]
        out = [dot_nn(pr, v_dups[kv]) for pr in probs]
        u_ref[0, :, SSM + 128 * pair : SSM + 128 * pair + 128] = jnp.where(
            left, out[0], out[1]
        ).astype(BF16)


def mix_backward_kernel(
    p_ref, gu_ref, segc_ref, segr_ref, conv_ref, head_ref, skip_ref,
    gp_ref, gconv_ref, ghead_ref, gskip_ref,
    mixed_ref, act_ref, gact_ref, colq_ref,
):
    allowed, links = block_masks(segc_ref[0], segr_ref[0])
    convolve(p_ref, conv_ref, links, mixed_ref, act_ref)
    raw, dt, decay, cum = steps_and_sums(p_ref, head_ref)
    dt_t, cum_t = dt.T, cum.T
    lanes = iota((T, 128), 1)
    left = lanes < HEAD_WIDTH
    b_rows = act_ref[:, SSM : SSM + STATE]
    c_rows = act_ref[:, SSM + STATE :]
    cb = dot_nt(c_rows, b_rows)
    gcb = jnp.zeros((T, T), F32)
    row_form = jnp.zeros((T, 128), F32)
    colq_ref[...] = jnp.zeros_like(colq_ref)
    for pair in range(MHEADS // 2):
        sl = slice(128 * pair, 128 * pair + 128)
        xs = act_ref[:, sl]
        xs16 = xs.astype(BF16)
        z = p_ref[0, :, sl]
        gm = gu_ref[0, :, sl]
        sg = jax.nn.sigmoid(z)
        gy = gm * (z * sg)
        gy16 = gy.astype(BF16)
        ys, gxs = [], []
        for h, keep in ((2 * pair, left), (2 * pair + 1, ~left)):
            decayed = jnp.exp(jnp.where(allowed, cum[:, h : h + 1] - cum_t[h : h + 1, :], -1e30))
            dt_row = dt_t[h : h + 1, :]
            base = decayed * cb
            k16 = (base * dt_row).astype(BF16)
            ys.append(dot_nn(k16, xs16))
            gxs.append(dot_tn(k16, gy16))
            gk = dot_nt(jnp.where(keep, gy, 0.0), xs16)
            gcb = gcb + gk * (decayed * dt_row)
            q = gk * base
            colq_ref[h : h + 1, :] = jnp.sum(q, 0, keepdims=True)
            row_form = jnp.where(lanes == h, jnp.sum(q * dt_row, 1, keepdims=True), row_form)
        skip = skip_ref[0:1, sl]
        y = jnp.where(left, ys[0], ys[1]) + skip * xs
        gp_ref[0, :, sl] = (gm * y * (sg * (1.0 + z * (1.0 - sg)))).astype(BF16)
        gact_ref[:, sl] = jnp.where(left, gxs[0], gxs[1]) + skip * gy
        gskip_ref[0, 0:1, sl] = jnp.sum(gy * xs, 0, keepdims=True)
    gact_ref[:, SSM : SSM + STATE] = dot_tn(gcb, c_rows)
    gact_ref[:, SSM + STATE :] = dot_nn(gcb, b_rows)
    col_form = colq_ref[...].T
    gcum = row_form - col_form * dt
    upper = jnp.where(iota((T, T), 0) <= iota((T, T), 1), 1.0, 0.0)
    gdecay = exact_dot(upper, gcum)
    gdt = col_form - gdecay * jnp.exp(head_ref[1:2, :])
    graw = jnp.where(lanes < MHEADS, gdt * jax.nn.sigmoid(raw), 0.0)
    gp_ref[0, :, OFF_R:PAD] = graw.astype(BF16)
    ghead_ref[0, 0:1, :] = jnp.sum(graw, 0, keepdims=True)
    ghead_ref[0, 1:2, :] = jnp.sum(gdecay * decay, 0, keepdims=True)
    for at in range(0, CH, 128):
        sl = slice(at, at + 128)
        mixed = mixed_ref[:, sl]
        sg = jax.nn.sigmoid(mixed)
        gmix = gact_ref[:, sl] * (sg * (1.0 + mixed * (1.0 - sg)))
        c = p_ref[0, :, SSM + at : SSM + at + 128]
        gc = gmix * conv_ref[0:1, sl]
        gconv_ref[0, 0:1, sl] = jnp.sum(gmix * c, 0, keepdims=True)
        for j in range(1, CONV):
            linked = gmix * links[j - 1]
            gc = gc + pltpu.roll(linked, T - j, 0) * conv_ref[j : j + 1, sl]
            gconv_ref[0, j : j + 1, sl] = jnp.sum(linked * pltpu.roll(c, j, 0), 0, keepdims=True)
        gconv_ref[0, 4:5, sl] = jnp.sum(gmix, 0, keepdims=True)
        gp_ref[0, :, SSM + at : SSM + at + 128] = gc.astype(BF16)
    k_dups = doubled(p_ref[0, :, OFF_K:OFF_V], left)
    v_dups = doubled(p_ref[0, :, OFF_V:OFF_R], left)
    gks, gvs = [], []
    for kv in range(KVHEADS):
        gk_sum = jnp.zeros((T, 128), F32)
        gv_sum = jnp.zeros((T, 128), F32)
        for pair in (2 * kv, 2 * kv + 1):
            sl = slice(OFF_Q + 128 * pair, OFF_Q + 128 * pair + 128)
            q_tile = p_ref[0, :, sl]
            go = gu_ref[0, :, SSM + 128 * pair : SSM + 128 * pair + 128]
            gq, gk, gv = [], [], []
            for keep in (left, ~left):
                probs = attention_probs(q_tile, keep, k_dups[kv], allowed)
                gpr = dot_nt(jnp.where(keep, go, 0.0), v_dups[kv])
                gs = probs * (gpr - jnp.sum(gpr * probs, -1, keepdims=True))
                gs = (gs * (1.0 / math.sqrt(HEAD_WIDTH))).astype(BF16)
                gq.append(dot_nn(gs, k_dups[kv]))
                gk.append(dot_tn(gs, q_tile))
                gv.append(dot_tn(probs, go))
            gp_ref[0, :, sl] = jnp.where(left, gq[0], gq[1]).astype(BF16)
            gk_sum = gk_sum + jnp.where(left, gk[0], gk[1])
            gv_sum = gv_sum + jnp.where(left, gv[0], gv[1])
        gks.append(gk_sum + pltpu.roll(gk_sum, HEAD_WIDTH, 1))
        gvs.append(gv_sum + pltpu.roll(gv_sum, HEAD_WIDTH, 1))
    gp_ref[0, :, OFF_K:OFF_V] = jnp.where(left, gks[0], gks[1]).astype(BF16)
    gp_ref[0, :, OFF_V:OFF_R] = jnp.where(left, gvs[0], gvs[1]).astype(BF16)


def whole(shape):
    return pl.BlockSpec(shape, lambda m: (0,) * len(shape))


def per_block(shape):
    return pl.BlockSpec((1, *shape), lambda m: (m,) + (0,) * len(shape))


def small_specs():
    return [
        per_block((T, 128)), per_block((8, T)), whole((8, CH)), whole((8, 128)), whole((8, SSM)),
    ]


def mix_forward(projected, tables):
    blocks = projected.shape[0]
    return pl.pallas_call(
        mix_forward_kernel,
        grid=(blocks,),
        in_specs=[per_block((T, PAD)), *small_specs()],
        out_specs=per_block((T, UW)),
        out_shape=jax.ShapeDtypeStruct((blocks, T, UW), BF16),
        scratch_shapes=[pltpu.VMEM((T, CH), F32)],
        compiler_params=pltpu.CompilerParams(vmem_limit_bytes=32 * 1024 * 1024),
        name="mix_forward",
    )(projected, *tables)


def mix_backward(projected, grad_joined, tables):
    blocks = projected.shape[0]
    return pl.pallas_call(
        mix_backward_kernel,
        grid=(blocks,),
        in_specs=[per_block((T, PAD)), per_block((T, UW)), *small_specs()],
        out_specs=[per_block((T, PAD)), per_block((8, CH)), per_block((8, 128)), per_block((8, SSM))],
        out_shape=[
            jax.ShapeDtypeStruct((blocks, T, PAD), BF16),
            jax.ShapeDtypeStruct((blocks, 8, CH), F32),
            jax.ShapeDtypeStruct((blocks, 8, 128), F32),
            jax.ShapeDtypeStruct((blocks, 8, SSM), F32),
        ],
        scratch_shapes=[
            pltpu.VMEM((T, CH), F32),
            pltpu.VMEM((T, CH), F32),
            pltpu.VMEM((T, CH), F32),
            pltpu.VMEM((128, T), F32),
        ],
        compiler_params=pltpu.CompilerParams(vmem_limit_bytes=40 * 1024 * 1024),
        name="mix_backward",
    )(projected, grad_joined, *tables)


def mixer_tables(segments, conv_rows, head_table):
    blocks = segments.shape[0]
    marks = segments.astype(F32)
    segc = jnp.broadcast_to(marks[:, :, None], (blocks, T, 128))
    segr = jnp.broadcast_to(marks[:, None, :], (blocks, 8, T))
    conv_rows = jnp.pad(conv_rows, ((0, 3), (0, 0)))
    head_rows = jnp.pad(head_table.T, ((0, 5), (0, 128 - MHEADS)))
    skip_rows = jnp.broadcast_to(jnp.repeat(head_table[:, 2], HEAD_WIDTH)[None], (8, SSM))
    return segc, segr, conv_rows, head_rows, skip_rows


MESH = pl.DeviceIdType.MESH
HOPS = ("xa", "xb", "za", "zb", "y")
ORDERS = (
    ("xa", "xb", "zb", "za", "y"),
    ("xb", "xa", "y", "zb", "za"),
    ("za", "zb", "xa", "y", "xb"),
    ("zb", "y", "za", "xb", "xa"),
    ("y", "za", "xb", "xa", "zb"),
)


def cut(array, tiles, orders=(0, 1, 2, 3, 4), first=0):
    parts = []
    for width, order in zip(tiles, orders):
        parts.append((array, 128 * first, 128 * width, ORDERS[order]))
        first += width
    return parts


GATHERED = (
    *cut(0, (7, 7, 7, 6, 5)),
    *cut(0, (1,), (4,), 32),
    *cut(1, (2, 3, 3), (2, 3, 4)),
    *cut(2, (7, 7, 6, 6, 6)),
    *cut(3, (3, 3, 2)),
)
SCATTERED = (
    *cut(3, (3, 3, 2)),
    *cut(1, (2, 3, 3), (2, 3, 4)),
    *cut(2, (7, 7, 6, 6, 6)),
    *cut(0, (7, 7, 7, 6, 6)),
    *cut(0, (1,), (4,), 33),
)
TAIL = 2 * FF
EXTRA = PAD
SHARD_ROWS = (64, 128, 64, 128)
SHARD_COLS = (PAD, 1024, 2 * FF, 1024)
SUM_COLS = (PAD + 128, 1024, 2 * FF, 1024)


def pair_a(i):
    return i + 1 - 2 * (i % 2)


def pair_b(i):
    return (i + 2 * (i % 2) + 3) % 4


def place():
    shard = lax.axis_index("shard")
    return lax.axis_index("section"), shard // 8, (shard // 2) % 4, shard % 2, lax.axis_index("rep")


def neighbours(section, y, z, core, x):
    def at(y, z, core, x):
        return (section, y * 8 + z * 2 + core, x)

    return {
        "core": at(y, z, 1 - core, x),
        "xa": at(y, z, core, pair_a(x)),
        "xb": at(y, z, core, pair_b(x)),
        "za": at(y, pair_a(z), core, x),
        "zb": at(y, pair_b(z), core, x),
        "y": at(1 - y, z, core, x),
        "xo": at(y, z, core, (x + 2) % 4),
    }


def meet(devices):
    barrier = pltpu.get_barrier_semaphore()
    for device in devices:
        pl.semaphore_signal(barrier, inc=1, device_id=device, device_id_type=MESH)
    pl.semaphore_wait(barrier, len(devices))


def halve(kept, hop, me):
    near, other = (pair_a, pair_b) if hop == "a" else (pair_b, pair_a)
    if kept[0][1] != 4:
        return [(near(me), 1)], [(me, 1)]
    if hop == "b":
        return [(2 * (near(me) // 2), 2)], [(2 * (me // 2), 2)]
    return [(near(me), 1), (other(near(me)), 1)], [(me, 1), (other(me), 1)]


def schedule(order, me_y, me_z, me_x):
    ys, zs, xs = [(0, 2)], [(0, 4)], [(0, 4)]
    stages = []
    for hop in order:
        if hop == "y":
            sent, ys = [(1 - me_y, 1)], [(me_y, 1)]
            gone = sent, zs, xs
        elif hop[0] == "z":
            sent, zs = halve(zs, hop[1], me_z)
            gone = ys, sent, xs
        else:
            sent, xs = halve(xs, hop[1], me_x)
            gone = ys, zs, sent
        stages.append((list(itertools.product(*gone)), list(itertools.product(ys, zs, xs))))
    return stages


def window(piece, quarter, column, columns):
    (y, ny), (z, nz), (x, nx) = piece
    rows = 0 if nx == 4 else pl.multiple_of(x * quarter, nx * quarter)
    return pl.ds(y, ny), pl.ds(z, nz), pl.ds(rows, nx * quarter), pl.ds(column, columns)


def piece_dims(piece, quarter):
    (_, ny), (_, nz), (_, nx) = piece
    return ny, nz, nx * quarter


def stage_shapes(parts):
    shapes = []
    for array, column, columns, order in parts:
        for sent, _ in schedule(order, 0, 0, 0):
            dims = piece_dims(sent[0], SHARD_ROWS[array] // 4)
            shapes.append((len(sent), *dims, columns))
    return shapes


def add_into(acc, window_at, arrived):
    ny, nz, rows, _ = arrived.shape
    ys, zs, rs, cs = window_at

    def step(i, carry):
        y, z = i // nz, i % nz
        at = (ys.start + y, zs.start + z, rs, cs)
        acc[at] = acc[at] + arrived[y, z]
        return carry

    if ny * nz == 1:
        step(0, 0)
    else:
        lax.fori_loop(0, ny * nz, step, 0)


def scatter_kernel(*refs):
    grads, extra, outs, smalls = refs[:4], refs[4], refs[5:9], refs[9:12]
    accs, wholes, cores = refs[12:16], refs[16:20], refs[20 : 20 + len(SCATTERED)]
    arrivals = refs[20 + len(SCATTERED) : -7]
    local_sem, core_send, core_recv, send_sem, recv_sem, last_send, last_recv = refs[-7:]
    section, y, z, core, x = place()
    near = neighbours(section, y, z, core, x)
    meet([near[name] for name in ("core", *HOPS, "xo")])

    loads, swaps = [], []
    for p, (array, column, columns, _) in enumerate(SCATTERED):
        cols = pl.ds(column, columns)
        grad = extra if (array, column) == (0, EXTRA) else grads[array].at[:, :, :, :, cols]
        swap = pltpu.make_async_remote_copy(
            src_ref=grad.at[:, :, 1 - core],
            dst_ref=cores[p],
            send_sem=core_send.at[p],
            recv_sem=core_recv.at[p],
            device_id=near["core"],
            device_id_type=MESH,
        )
        swap.start()
        load = pltpu.make_async_copy(
            grad.at[:, :, core], accs[array].at[:, :, :, cols], local_sem.at[p]
        )
        load.start()
        swaps.append(swap)
        loads.append(load)

    plans = [schedule(order, y, z, x) for _, _, _, order in SCATTERED]
    flying = {}
    sems = 0
    for stage in range(len(HOPS) + 1):
        for p, (array, column, columns, order) in enumerate(SCATTERED):
            quarter = SHARD_ROWS[array] // 4
            if stage == 0:
                loads[p].wait()
                swaps[p].wait_recv()
                add_into(accs[array], window(((0, 2), (0, 4), (0, 4)), quarter, column, columns), cores[p])
            else:
                kept = plans[p][stage - 1][1]
                for k, (copy, piece) in enumerate(zip(flying[p, stage - 1], kept)):
                    copy.wait_recv()
                    add_into(
                        accs[array],
                        window(piece, quarter, column, columns),
                        arrivals[p * len(HOPS) + stage - 1].at[k],
                    )
            if stage < len(HOPS):
                copies = []
                for k, piece in enumerate(plans[p][stage][0]):
                    copy = pltpu.make_async_remote_copy(
                        src_ref=accs[array].at[window(piece, quarter, column, columns)],
                        dst_ref=arrivals[p * len(HOPS) + stage].at[k],
                        send_sem=send_sem.at[sems],
                        recv_sem=recv_sem.at[sems],
                        device_id=near[order[stage]],
                        device_id_type=MESH,
                    )
                    copy.start()
                    copies.append(copy)
                    sems += 1
                flying[p, stage] = copies

    last = []
    for array in range(4):
        quarter = SHARD_ROWS[array] // 4
        mine = pl.ds(pl.multiple_of(x * quarter, quarter), quarter)
        for k, name in enumerate(("xo", "xa", "xb")):
            copy = pltpu.make_async_remote_copy(
                src_ref=accs[array].at[y, z, mine],
                dst_ref=wholes[array].at[mine],
                send_sem=last_send.at[array, k],
                recv_sem=last_recv.at[array, k],
                device_id=near[name],
                device_id_type=MESH,
            )
            copy.start()
            last.append(copy)
        wholes[array][mine, :] = accs[array][y, z, mine, :]
    for array in range(4):
        for k in range(3):
            last[array * 3 + k].wait_recv()
        outs[array][...] = wholes[array][:, : outs[array].shape[1]].astype(F32)
    small = wholes[0][:, EXTRA:].astype(F32)
    out_gains, out_conv, out_head = smalls
    out_gains[...] = small[:, :2]
    out_conv[:56, :] = small[:56, 2 : 3 + CONV]
    out_conv[56:, :] = small[:56, 3 + CONV : 4 + 2 * CONV]
    out_head[...] = small[:MHEADS, 12:15]
    for copy in last + swaps + [c for copies in flying.values() for c in copies]:
        copy.wait_send()


def scatter_sums(grads, extra):
    n_copies = sum(shape[0] for shape in stage_shapes(SCATTERED))
    n_parts = len(SCATTERED)
    out_shapes = [
        (64, PIN), (128, 1024), (64, 2 * FF), (128, 1024), (64, 2), (112, CONV + 1), (MHEADS, 3),
    ]
    return pl.pallas_call(
        scatter_kernel,
        in_specs=[pl.BlockSpec(memory_space=pl.ANY)] * 5,
        out_specs=[pl.BlockSpec(memory_space=pltpu.VMEM)] * 7,
        out_shape=[jax.ShapeDtypeStruct(s, F32) for s in out_shapes],
        scratch_shapes=[
            *[pltpu.VMEM((2, 4, r, c), BF16) for r, c in zip(SHARD_ROWS, SUM_COLS)],
            *[pltpu.VMEM((r, c), BF16) for r, c in zip(SHARD_ROWS, SUM_COLS)],
            *[pltpu.VMEM((2, 4, SHARD_ROWS[a], cols), BF16) for a, _, cols, _ in SCATTERED],
            *[pltpu.VMEM(shape, BF16) for shape in stage_shapes(SCATTERED)],
            pltpu.SemaphoreType.DMA((n_parts,)),
            pltpu.SemaphoreType.DMA((n_parts,)),
            pltpu.SemaphoreType.DMA((n_parts,)),
            pltpu.SemaphoreType.DMA((n_copies,)),
            pltpu.SemaphoreType.DMA((n_copies,)),
            pltpu.SemaphoreType.DMA((4, 3)),
            pltpu.SemaphoreType.DMA((4, 3)),
        ],
        compiler_params=pltpu.CompilerParams(
            collective_id=1, has_side_effects=True, vmem_limit_bytes=58 * 1024 * 1024
        ),
        name="scatter_sums",
    )(*grads, extra)


def gather_kernel(*refs):
    shards, tail, outs = refs[:4], refs[4], refs[5:9]
    local_sem, send_sem, recv_sem, core_send, core_recv = refs[9:]
    section, y, z, core, x = place()
    near = neighbours(section, y, z, core, x)
    meet([near[name] for name in ("core", *HOPS)])

    def at(array, piece, column, columns):
        ys, zs, rows, cols = window(piece, SHARD_ROWS[array] // 4, column, columns)
        return outs[array].at[ys, zs, pl.ds(core, 1), rows, cols]

    def own(array, column, columns):
        quarter = SHARD_ROWS[array] // 4
        rows = pl.ds(pl.multiple_of(x * quarter, quarter), quarter)
        if (array, column) == (0, TAIL):
            return tail.at[:, :, :, rows]
        return shards[array].at[:, :, :, rows, pl.ds(column, columns)]

    passed = []

    def pass_on(source, target):
        k = len(passed)
        copy = pltpu.make_async_remote_copy(
            src_ref=source,
            dst_ref=target,
            send_sem=core_send.at[k],
            recv_sem=core_recv.at[k],
            device_id=near["core"],
            device_id_type=MESH,
        )
        copy.start()
        passed.append(copy)

    locals_ = []
    for p, (array, column, columns, _) in enumerate(GATHERED):
        copy = pltpu.make_async_copy(
            own(array, column, columns), at(array, ((y, 1), (z, 1), (x, 1)), column, columns), local_sem.at[p]
        )
        copy.start()
        locals_.append(copy)

    plans = [schedule(order, y, z, x)[::-1] for _, _, _, order in GATHERED]
    flying, sent = {}, []
    for stage in range(len(HOPS) + 1):
        for p, (array, column, columns, order) in enumerate(GATHERED):
            if stage:
                for copy in flying[p, stage - 1]:
                    copy.wait_recv()
            if stage == 1:
                locals_[p].wait()
            if stage < len(HOPS):
                copies = []
                for piece in plans[p][stage][1]:
                    target = at(array, piece, column, columns)
                    copy = pltpu.make_async_remote_copy(
                        src_ref=target if stage else own(array, column, columns),
                        dst_ref=target,
                        send_sem=send_sem.at[len(sent)],
                        recv_sem=recv_sem.at[len(sent)],
                        device_id=near[order[::-1][stage]],
                        device_id_type=MESH,
                    )
                    copy.start()
                    copies.append(copy)
                    sent.append(copy)
                flying[p, stage] = copies
            if stage:
                for piece in plans[p][stage - 1][0]:
                    here = at(array, piece, column, columns)
                    pass_on(here, here)
            else:
                pass_on(own(array, column, columns), at(array, ((y, 1), (z, 1), (x, 1)), column, columns))
    for copy in passed:
        copy.wait()
    for copy in sent:
        copy.wait_send()


def gather_shards(shards, tail):
    n_copies = sum(shape[0] for shape in stage_shapes(GATHERED))
    n_passed = n_copies + len(GATHERED)
    return pl.pallas_call(
        gather_kernel,
        in_specs=[pl.BlockSpec(memory_space=pl.ANY)] * 5,
        out_specs=[pl.BlockSpec(memory_space=pl.ANY)] * 4,
        out_shape=[
            jax.ShapeDtypeStruct((2, 4, 2, r, c), BF16) for r, c in zip(SHARD_ROWS, SHARD_COLS)
        ],
        scratch_shapes=[
            pltpu.SemaphoreType.DMA((len(GATHERED),)),
            pltpu.SemaphoreType.DMA((n_copies,)),
            pltpu.SemaphoreType.DMA((n_copies,)),
            pltpu.SemaphoreType.DMA((n_passed,)),
            pltpu.SemaphoreType.DMA((n_passed,)),
        ],
        compiler_params=pltpu.CompilerParams(collective_id=2, has_side_effects=True),
        name="gather_shards",
    )(*shards, tail)


def rms_norm(values, gain):
    return values * lax.rsqrt(jnp.mean(values * values, -1, keepdims=True) + 1e-05) * gain


def rms_back(values, gain, grad):
    scale = lax.rsqrt(jnp.mean(values * values, -1, keepdims=True) + 1e-05)
    unit = values * scale
    scaled = grad * gain
    grad_values = scale * (scaled - unit * jnp.mean(scaled * unit, -1, keepdims=True))
    return grad_values, jnp.sum(grad * unit, 0)


def forward_product(left, weight):
    return jnp.dot(left, weight, preferred_element_type=F32)


def back_product(grad_rows, weight):
    return lax.dot_general(
        grad_rows, weight, (((1,), (1,)), ((), ())), preferred_element_type=F32
    )


def outer_sum(left, right):
    return lax.dot_general(
        left, right, (((0,), (0,)), ((), ())), preferred_element_type=F32
    ).astype(BF16)


def layer_forward(inputs, weights, tables):
    gains, w_in, w_out, w_gate_up, w_down = weights
    blocks = inputs.shape[0] // T
    normed = rms_norm(inputs, gains[0]).astype(BF16)
    projected = forward_product(normed, w_in)
    joined = mix_forward(projected.reshape(blocks, T, PAD), tables).reshape(blocks * T, UW)
    hidden = inputs + forward_product(joined, w_out)
    normed_two = rms_norm(hidden, gains[1]).astype(BF16)
    gate_up = forward_product(normed_two, w_gate_up)
    activated = (jax.nn.silu(gate_up[:, :FF]) * gate_up[:, FF:]).astype(BF16)
    result = hidden + forward_product(activated, w_down)
    return result, (inputs, normed, projected, joined, hidden, normed_two, gate_up, activated)


def layer_backward(grad_out, saved, weights, tables):
    gains, w_in, w_out, w_gate_up, w_down = weights
    inputs, normed, projected, joined, hidden, normed_two, gate_up, activated = saved
    blocks = inputs.shape[0] // T
    grad_ffn = grad_out.astype(BF16)
    grad_act = back_product(grad_ffn, w_down)
    gate, up = gate_up[:, :FF], gate_up[:, FF:]
    sig = jax.nn.sigmoid(gate)
    grad_gate = (grad_act * up * (sig * (1.0 + gate * (1.0 - sig)))).astype(BF16)
    grad_up = (grad_act * (gate * sig)).astype(BF16)
    grad_gate_up = jnp.concatenate([grad_gate, grad_up], 1)
    grad_hidden, grad_gain_two = rms_back(hidden, gains[1], back_product(grad_gate_up, w_gate_up))
    grad_hidden = grad_out + grad_hidden
    grad_branch = grad_hidden.astype(BF16)
    grad_joined = back_product(grad_branch, w_out)
    grad_proj, grad_conv, grad_head, grad_skip = mix_backward(
        projected.reshape(blocks, T, PAD), grad_joined.reshape(blocks, T, UW), tables
    )
    grad_proj = grad_proj.reshape(blocks * T, PAD)
    grad_input, grad_gain_one = rms_back(inputs, gains[0], back_product(grad_proj, w_in))
    grad_input = grad_hidden + grad_input
    pairs = (
        (normed, grad_proj),
        (joined, grad_branch),
        (normed_two, grad_gate_up),
        (activated, grad_ffn),
    )
    return grad_input, pairs, (grad_gain_one, grad_gain_two, grad_conv, grad_head, grad_skip)


def across(array, by):
    return lax.ppermute(array, "section", [(0, 1)] if by > 0 else [(1, 0)])


def split_conv(table):
    parts = table.reshape(-1, 2, 56, CONV + 1).transpose(0, 2, 1, 3).reshape(-1, 56, 2 * (CONV + 1))
    return jnp.pad(parts, ((0, 0), (0, 8), (0, 0))).reshape(-1, 2 * (CONV + 1))


def join_conv(parts):
    parts = parts[:, :56].reshape(-1, 56, 2, CONV + 1)
    return parts.transpose(3, 0, 2, 1).reshape(CONV + 1, -1)


def gather_weights(norm_gains, w_in, conv_params, w_out, w_gate_up, w_down):
    filler = jnp.zeros((w_in.shape[0], PAD - PIN - 12), BF16)
    tail = jnp.concatenate([w_in[:, TAIL:], norm_gains, split_conv(conv_params), filler], 1)
    parts = gather_shards(
        [a.reshape(1, 1, 1, *a.shape) for a in (w_in, w_out, w_gate_up, w_down)],
        tail.reshape(1, 1, 1, *tail.shape),
    )
    small = parts[0][..., PIN : PIN + 12].reshape(16, 64, 12).astype(F32)
    gains = small[:, :, :2].reshape(-1, 2).T
    return (gains, *[a.reshape(-1, a.shape[-1]) for a in parts]), join_conv(small[:, :, 2:])


def body(
    tokens,
    segment_ids,
    cotangent,
    norm_gains,
    w_in,
    conv_params,
    head_params,
    w_out,
    w_gate_up,
    w_down,
):
    section = lax.axis_index("section")
    blocks, _, width = tokens.shape
    rows = blocks * T
    weights, conv_rows = gather_weights(
        norm_gains[0], w_in[0], conv_params[0], w_out[0], w_gate_up[0], w_down[0]
    )
    tables = mixer_tables(segment_ids[:, 0], conv_rows, head_params[0].astype(F32))

    own = tokens.reshape(rows, width)
    first, _ = layer_forward(own.astype(F32), weights, tables)
    received = across(first.astype(BF16), 1)
    inputs = jnp.where(section == 0, own, received).astype(F32)
    result, saved = layer_forward(inputs, weights, tables)

    top = cotangent.reshape(rows, width)
    first_grad, _, _ = layer_backward(top.astype(F32), saved, weights, tables)
    coming = across(first_grad.astype(BF16), -1)
    grad_out = jnp.where(section == 1, top, coming).astype(F32)
    grad_input, pairs, smalls = layer_backward(grad_out, saved, weights, tables)

    grad_gain_one, grad_gain_two, grad_conv, grad_head, grad_skip = smalls
    sums = [outer_sum(left, right) for left, right in pairs]
    shards = lax.axis_size("shard")
    gains = jnp.stack([grad_gain_one, grad_gain_two], 1)
    conv = split_conv(jnp.sum(grad_conv, 0)[: CONV + 1].T)
    head = jnp.sum(grad_head, 0)[:2, :MHEADS]
    skip = jnp.sum(jnp.sum(grad_skip, 0)[0].reshape(MHEADS, HEAD_WIDTH), 1)
    head = jnp.pad(jnp.concatenate([head, skip[None]], 0).T, ((0, 64 - MHEADS), (0, 0)))
    head = jnp.broadcast_to(head[None], (shards, 64, 3)).reshape(shards * 64, 3)
    extra = jnp.concatenate([gains, conv, head], 1)
    extra = jnp.pad(extra, ((0, 0), (0, 128 - extra.shape[1]))).astype(BF16)
    out_in, out_out, out_gu, out_dn, out_gains, out_conv, out_head = scatter_sums(
        [g.reshape(2, 4, 2, g.shape[0] // 16, g.shape[1]) for g in sums],
        extra.reshape(2, 4, 2, 64, 128),
    )
    return (
        result.astype(BF16).reshape(1, blocks, T, width),
        grad_input.reshape(1, blocks, T, width),
        out_gains[None],
        out_in[None],
        out_conv[None],
        out_head[None],
        out_out[None],
        out_gu[None],
        out_dn[None],
    )


def solution(mesh):
    in_specs = (
        P(None, ("shard", "rep"), None),
        P(None, ("shard", "rep"), None),
        P(None, ("shard", "rep"), None),
        P("section", "shard", None),
        P("section", "shard", None),
        P("section", "shard", None),
        P("section", None, None),
        P("section", "shard", None),
        P("section", "shard", None),
        P("section", "shard", None),
    )
    out_specs = (
        P("section", None, ("shard", "rep"), None),
        P("section", None, ("shard", "rep"), None),
        P("section", "shard", None),
        P("section", "shard", None),
        P("section", "shard", None),
        P("section", None, None),
        P("section", "shard", None),
        P("section", "shard", None),
        P("section", "shard", None),
    )
    return jax.shard_map(body, mesh=mesh, in_specs=in_specs, out_specs=out_specs, check_vma=False)
```

profile of v0, /device:TPU:1, one launch (start us, length us, event | category | flops | bytes accessed | tf_op | source)
XLA Modules:
  0.0 338.4 jit_solution(16082361567238604369)
XLA Ops:
  6.6 78.0 %gather_shards.1 = (bf16[2,4,2,64,4224]{4,3,2,1,0:T(8,128)(2,1)}, bf16[2,4,2,128,1024]{4,3,2,1,0:T(8,128)(2,1)}, bf16[2,4,2,64,4096]{4,3,2,1,0:T(8,128)(2,1)}, bf16[2,4,2,128,1024]{4,3,2,1,0:T(8,128)(2,1)}) custom-call(bf16[1,1,1,64,4120]{4,3,2,1,0:T(8,128)(2,1)} %bitcast.171, bf16[1,1,1,128,1024]{4,3,2,1,0:T(8,128)(2,1)} %bitcast.181, ...), custom_call_target="tpu_custom_call" | custom-call | tf_op jit(solution)/shard_map/gather_shards/pallas_call | solution.py:637
  86.6 5.7 %fusion.35.p_ref = f32[2,112,4224]{2,1,0:T(8,128)S(1)} fusion(bf16[1024,4224,1]{1,0,2:T(8,128)(2,1)} %bitcast.137, bf16[2,112,1024]{2,1,0:T(8,128)(2,1)S(1)} %copy-done.6, f32[1024]{0:T(1024)S(1)} %bitcast.175, f32[2,112]{1,0:T(2,128)S(1)} %add_rsqrt_fusion.3), kind=kOutput, calls=%fused_computation.64 | convolution fusion | flops 1938685952 | bytes 12899200 | tf_op jit(solution)/shard_map/dot_general | solution.py:669
  92.5 6.1 %mix_forward.2 = bf16[2,112,2048]{2,1,0:T(8,128)(2,1)S(1)} custom-call(f32[2,112,4224]{2,1,0:T(8,128)S(1)} %fusion.35.p_ref, f32[2,112,128]{2,1,0:T(8,128)S(1)} %broadcast_in_dim.31.segc_ref, f32[2,8,112]{2,1,0:T(8,128)S(1)} %broadcast_in_dim.32.segr_ref, f32[8,1792]{1,0:T(8,128)S(1)} %pad.27.conv_ref, f32[8,128]{1,0:T(8,128)S(1)} %pad.28.head_ref, ...), custom_call_target="tpu_custom_call" | custom-call | tf_op jit(solution)/shard_map/mix_forward/pallas_call | solution.py:247
  99.8 5.7 %fusion.34 = f32[224,4096]{1,0:T(8,128)S(1)} fusion(bf16[1024,4096]{1,0:T(8,128)(2,1)} %bitcast.128, f32[224,1024]{1,0:T(8,128)S(1)} %get-tuple-element.93, f32[1024]{0:T(1024)S(1)} %bitcast.162, f32[224]{0:T(256)S(1)} %add_rsqrt_fusion.2), kind=kOutput, calls=%fused_computation.63 | convolution fusion | flops 1879736320 | bytes 12981120 | tf_op jit(solution)/shard_map/dot_general | solution.py:669
  106.8 4.8 %collective-permute-start = (bf16[224,1024]{1,0:T(8,128)(2,1)S(1)}, bf16[224,1024]{1,0:T(8,128)(2,1)S(1)}, u32[]{:S(2)}, u32[]{:S(2)}) collective-permute-start(bf16[224,1024]{1,0:T(8,128)(2,1)S(1)} %fusion.15), channel_id=1, source_target_pairs={{0,64},{1,65},{2,66},{3,67},{4,68},{5,69},{6,70},{7,71},{8,72},{9,... | collective-permute-start | bytes 1376264 | tf_op jit(solution)/shard_map/ppermute | solution.py:729
  111.6 9.7 %collective-permute-done = bf16[224,1024]{1,0:T(8,128)(2,1)S(1)} collective-permute-done((bf16[224,1024]{1,0:T(8,128)(2,1)S(1)}, bf16[224,1024]{1,0:T(8,128)(2,1)S(1)}, u32[]{:S(2)}, u32[]{:S(2)}) %collective-permute-start) | collective-permute-done | bytes 458784 | tf_op jit(solution)/shard_map/ppermute | solution.py:729
  121.8 5.8 %fusion.51.p_ref = f32[2,112,4224]{2,1,0:T(8,128)S(1)} fusion(bf16[2,112,1024]{2,1,0:T(8,128)(2,1)S(1)} %bitcast.152, bf16[1024,4224,1]{1,0,2:T(8,128)(2,1)} %bitcast.138), kind=kOutput, calls=%fused_computation.100 | convolution fusion | flops 1937768448 | bytes 12894208 | tf_op jit(solution)/shard_map/dot_general | solution.py:669
  127.6 6.1 %mix_forward.3 = bf16[2,112,2048]{2,1,0:T(8,128)(2,1)S(1)} custom-call(f32[2,112,4224]{2,1,0:T(8,128)S(1)} %fusion.51.p_ref, f32[2,112,128]{2,1,0:T(8,128)S(1)} %broadcast_in_dim.31.segc_ref, f32[2,8,112]{2,1,0:T(8,128)S(1)} %broadcast_in_dim.32.segr_ref, f32[8,1792]{1,0:T(8,128)S(1)} %pad.27.conv_ref, f32[8,128]{1,0:T(8,128)S(1)} %pad.28.head_ref, ...), custom_call_target="tpu_custom_call" | custom-call | tf_op jit(solution)/shard_map/mix_forward/pallas_call | solution.py:247
  137.4 3.2 multiply_convert_fusion.3
  140.7 4.4 %multiply_reduce_fusion.2 = (f32[224]{0:T(256)S(1)}, f32[224,1024]{1,0:T(8,128)S(1)}) fusion(f32[224,1024]{1,0:T(8,128)S(1)} %get-tuple-element.95, f32[224]{0:T(256)S(1)} %add_rsqrt_fusion, f32[1024]{0:T(1024)S(1)} %bitcast.164, bf16[1024,4096]{1,0:T(8,128)(2,1)S(1)} %bitcast.132, bf16[224,2048]{1,0:T(8,128)(2,1)} %get-tuple-element.86, ...), kind=kOutput, calls=%fused_computation.58 | convolution fusion | flops 1883635456 | bytes 12064512 | tf_op jit(solution)/shard_map/dot_general | solution.py:673
  146.1 3.7 %fusion.52.gu_ref = f32[2,112,2048]{2,1,0:T(8,128)S(1)} fusion(bf16[2,112,1024]{2,1,0:T(8,128)(2,1)S(1)} %bitcast.158, bf16[2048,1024,1]{1,0,2:T(8,128)(2,1)} %bitcast.148), kind=kOutput, calls=%fused_computation.101 | convolution fusion | flops 939524096 | bytes 6488064 | tf_op jit(solution)/shard_map/dot_general | solution.py:673
  149.8 15.9 %mix_backward.2 = (bf16[2,112,4224]{2,1,0:T(8,128)(2,1)S(1)}, f32[2,8,1792]{2,1,0:T(8,128)}, f32[2,8,128]{2,1,0:T(8,128)}, f32[2,8,1536]{2,1,0:T(8,128)}) custom-call(f32[2,112,4224]{2,1,0:T(8,128)S(1)} %fusion.51.p_ref, f32[2,112,2048]{2,1,0:T(8,128)S(1)} %fusion.52.gu_ref, f32[2,112,128]{2,1,0:T(8,128)S(1)} %broadcast_in_dim.31.segc_ref, ...), custom_call_target="tpu_custom_call" | custom-call | tf_op jit(solution)/shard_map/mix_backward/pallas_call | solution.py:261
  165.8 2.8 fusion.22
  171.3 13.6 %collective-permute-done.1 = bf16[224,1024]{1,0:T(8,128)(2,1)} collective-permute-done((bf16[224,1024]{1,0:T(8,128)(2,1)}, bf16[224,1024]{1,0:T(8,128)(2,1)}, u32[]{:S(2)}, u32[]{:S(2)}) %collective-permute-start.1) | collective-permute-done | bytes 458784 | tf_op jit(solution)/shard_map/ppermute | solution.py:729
  186.1 5.3 %multiply_convert_fusion.1 = (bf16[224,2048]{1,0:T(8,128)(2,1)S(1)}, bf16[224,2048]{1,0:T(8,128)(2,1)S(1)}, bf16[224,2048]{1,0:T(8,128)(2,1)S(1)}) fusion(f32[224,4096]{1,0:T(8,128)} %copy-done.7, bf16[224,1024]{1,0:T(8,128)(2,1)S(1)} %broadcast_select_fusion, bf16[2048,1024]{1,0:T(8,128)(2,1)} %bitcast.194), kind=kOutput, calls=%fused_computation.13 | convolution fusion | flops 946405376 | bytes 11075584 | tf_op jit(solution)/shard_map/dot_general | solution.py:673
  193.4 3.2 convolution_convert_fusion.2
  196.6 2.9 multiply_reduce_fusion
  199.6 5.7 %convolution_convert_fusion.1 = bf16[1024,4096]{1,0:T(8,128)(2,1)} fusion(bf16[224,2048]{1,0:T(8,128)(2,1)S(1)} %get-tuple-element.84, bf16[224,2048]{1,0:T(8,128)(2,1)S(1)} %get-tuple-element.83, f32[224,1024]{1,0:T(8,128)S(1)} %get-tuple-element.95, f32[224]{0:T(256)S(1)} %add_rsqrt_fusion, f32[1024]{0:T(1024)S(1)} %bitcast.166), kind=kOutput, calls=%fused_computation.1 | convolution fusion | flops 1887600640 | bytes 11146112 | tf_op jit(solution)/shard_map/dot_general | solution.py:679
  205.6 3.5 %convolution_convert_fusion.3 = bf16[2048,1024]{1,0:T(8,128)(2,1)} fusion(bf16[224,2048]{1,0:T(8,128)(2,1)S(1)} %bitcast.123, bf16[224,1024]{1,0:T(8,128)(2,1)S(1)} %fusion.49), kind=kOutput, calls=%fused_computation.3 | convolution fusion | flops 941621248 | bytes 5570560 | tf_op jit(solution)/shard_map/dot_general | solution.py:679
  211.4 15.2 %mix_backward.3 = (bf16[2,112,4224]{2,1,0:T(8,128)(2,1)S(1)}, f32[2,8,1792]{2,1,0:T(8,128)S(1)}, f32[2,8,128]{2,1,0:T(8,128)S(1)}, f32[2,8,1536]{2,1,0:T(8,128)S(1)}) custom-call(f32[2,112,4224]{2,1,0:T(8,128)S(1)} %copy-done.1, f32[2,112,2048]{2,1,0:T(8,128)S(1)} %fusion.53.gu_ref, f32[2,112,128]{2,1,0:T(8,128)S(1)} %broadcast_in_dim.31.segc_ref, ...), custom_call_target="tpu_custom_call" | custom-call | tf_op jit(solution)/shard_map/mix_backward/pallas_call | solution.py:261
  226.6 3.6 %fusion.31 = (bf16[1024]{0:T(1024)(128)(2,1)S(1)}, f32[224]{0:T(256)S(1)}, f32[224,1024]{1,0:T(8,128)}) fusion(bf16[224,1024]{1,0:T(8,128)(2,1)S(1)} %get-tuple-element.82, f32[224]{0:T(256)S(1)} %add_rsqrt_fusion.1, f32[1024]{0:T(1024)S(1)} %bitcast.178, bf16[224,4224]{1,0:T(8,128)(2,1)S(1)} %bitcast.124, bf16[1024,4224]{1,0:T(8,128)(2,1)S(1)} %bitcast.144), kind=kOutput, calls=%fused_computation.52 | convolution fusion | flops 1939372800 | bytes 11927296 | tf_op jit(solution)/shard_map/dot_general | solution.py:673
  230.2 5.9 %convolution_convert_fusion = bf16[1024,4224]{1,0:T(8,128)(2,1)} fusion(bf16[224,1024]{1,0:T(8,128)(2,1)S(1)} %fusion.21, bf16[224,4224]{1,0:T(8,128)(2,1)S(1)} %bitcast.125), kind=kOutput, calls=%fused_computation | convolution fusion | flops 1942093824 | bytes 11001856 | tf_op jit(solution)/shard_map/dot_general | solution.py:679
  237.8 89.8 %scatter_sums.1 = (f32[64,4120]{1,0:T(8,128)}, f32[128,1024]{1,0:T(8,128)}, f32[64,4096]{1,0:T(8,128)}, f32[128,1024]{1,0:T(8,128)}, f32[64,2]{1,0:T(8,128)}, /*index=5*/f32[112,5]{1,0:T(8,128)}, f32[24,3]{1,0:T(8,128)}) custom-call(bf16[2,4,2,64,4224]{4,3,2,1,0:T(8,128)(2,1)} %bitcast.136, bf16[2,4,2,128,1024]{4,3,2,1,0:T(8,128)(2,1)} %bitcast.147, ...), custom_call_target="tpu_custom_call" | custom-call | tf_op jit(solution)/shard_map/scatter_sums/pallas_call | solution.py:531
  331.8 2.8 fusion.30
  (140 shorter events, 33.3 us)
Async XLA Ops:
  0.6 86.0 %copy-start.6 = (bf16[2,112,1024]{2,1,0:T(8,128)(2,1)S(1)}, bf16[2,112,1024]{2,1,0:T(8,128)(2,1)}, u32[]{:S(2)}) copy-start(bf16[2,112,1024]{2,1,0:T(8,128)(2,1)} %param.10) | copy-start | bytes 1376260
  92.4 6.2 %copy-start.2 = (bf16[2,4,2,128,1024]{4,3,2,1,0:T(8,128)(2,1)S(1)}, bf16[2,4,2,128,1024]{4,3,2,1,0:T(8,128)(2,1)}, u32[]{:S(2)}) copy-start(bf16[2,4,2,128,1024]{4,3,2,1,0:T(8,128)(2,1)} %get-tuple-element.26) | copy-start | bytes 12582916
  99.8 5.7 %copy-start.16 = (bf16[2,4,2,128,1024]{4,3,2,1,0:T(8,128)(2,1)S(1)}, bf16[2,4,2,128,1024]{4,3,2,1,0:T(8,128)(2,1)}, u32[]{:S(2)}) copy-start(bf16[2,4,2,128,1024]{4,3,2,1,0:T(8,128)(2,1)} %get-tuple-element.28) | copy-start | bytes 12582916
  106.8 14.6 %collective-permute-start = (bf16[224,1024]{1,0:T(8,128)(2,1)S(1)}, bf16[224,1024]{1,0:T(8,128)(2,1)S(1)}, u32[]{:S(2)}, u32[]{:S(2)}) collective-permute-start(bf16[224,1024]{1,0:T(8,128)(2,1)S(1)} %fusion.15), channel_id=1, source_target_pairs={{0,64},{1,65},{2,66},{3,67},{4,68},{5,69},{6,70},{7,71},{8,72},{9,... | collective-permute-start | bytes 1376264 | tf_op jit(solution)/shard_map/ppermute | solution.py:729
  121.6 13.5 %slice-start = ((s8[8388608]{0:T(1024)(128)(4,1)}), s8[4194304]{0:T(1024)(128)(4,1)S(1)}, s32[]{:S(2)}) async-start(s8[8388608]{0:T(1024)(128)(4,1)} %bitcast.129), calls=%async_computation | async-start | bytes 8388608
  121.8 13.3 %slice-start.1 = ((s8[8388608]{0:T(1024)(128)(4,1)}), s8[4194304]{0:T(1024)(128)(4,1)S(1)}, s32[]{:S(2)}) async-start(s8[8388608]{0:T(1024)(128)(4,1)} %bitcast.129), calls=%async_computation.1 | async-start | bytes 8388608
  127.6 22.2 %copy-start = (f32[2,112,4224]{2,1,0:T(8,128)}, f32[2,112,4224]{2,1,0:T(8,128)S(1)}, u32[]{:S(2)}) copy-start(f32[2,112,4224]{2,1,0:T(8,128)S(1)} %fusion.51.p_ref) | copy-start | bytes 11354116
  127.6 6.2 %copy-start.3 = (bf16[2,4,2,128,1024]{4,3,2,1,0:T(8,128)(2,1)S(1)}, bf16[2,4,2,128,1024]{4,3,2,1,0:T(8,128)(2,1)}, u32[]{:S(2)}) copy-start(bf16[2,4,2,128,1024]{4,3,2,1,0:T(8,128)(2,1)} %get-tuple-element.26) | copy-start | bytes 12582916
  137.3 3.4 %copy-start.7 = (f32[224,4096]{1,0:T(8,128)}, f32[224,4096]{1,0:T(8,128)S(1)}, u32[]{:S(2)}) copy-start(f32[224,4096]{1,0:T(8,128)S(1)} %fusion.47) | copy-start | bytes 11010052
  140.7 25.1 %slice-start.4 = ((s8[8650752]{0:T(1024)(128)(4,1)}), s8[4194304]{0:T(1024)(128)(4,1)S(1)}, s32[]{:S(2)}) async-start(s8[8650752]{0:T(1024)(128)(4,1)} %bitcast.139), calls=%async_computation.4 | async-start | bytes 8388608
  140.7 25.1 %slice-start.5 = ((s8[8650752]{0:T(1024)(128)(4,1)}), s8[262144]{0:T(1024)(128)(4,1)S(1)}, s32[]{:S(2)}) async-start(s8[8650752]{0:T(1024)(128)(4,1)} %bitcast.139), calls=%async_computation.5 | async-start | bytes 524288
  146.1 19.7 %slice-start.6 = ((s8[8650752]{0:T(1024)(128)(4,1)}), s8[4194304]{0:T(1024)(128)(4,1)S(1)}, s32[]{:S(2)}) async-start(s8[8650752]{0:T(1024)(128)(4,1)} %bitcast.139), calls=%async_computation.6 | async-start | bytes 8388608
  169.9 15.0 %collective-permute-start.1 = (bf16[224,1024]{1,0:T(8,128)(2,1)}, bf16[224,1024]{1,0:T(8,128)(2,1)}, u32[]{:S(2)}, u32[]{:S(2)}) collective-permute-start(bf16[224,1024]{1,0:T(8,128)(2,1)} %fusion.26), channel_id=1, source_target_pairs={{64,0},{65,1},{66,2},{67,3},{68,4},{69,5},{70,6},{71,7},{72,8},{73... | collective-permute-start | bytes 1376264 | tf_op jit(solution)/shard_map/ppermute | solution.py:729
  186.1 5.3 %copy-start.18 = (bf16[2,4,2,128,1024]{4,3,2,1,0:T(8,128)(2,1)S(1)}, bf16[2,4,2,128,1024]{4,3,2,1,0:T(8,128)(2,1)}, u32[]{:S(2)}) copy-start(bf16[2,4,2,128,1024]{4,3,2,1,0:T(8,128)(2,1)} %get-tuple-element.28) | copy-start | bytes 12582916
  191.4 5.2 %slice-start.2 = ((s8[8388608]{0:T(1024)(128)(4,1)}), s8[4194304]{0:T(1024)(128)(4,1)S(1)}, s32[]{:S(2)}) async-start(s8[8388608]{0:T(1024)(128)(4,1)} %bitcast.133), calls=%async_computation.2 | async-start | bytes 8388608
  193.4 3.3 slice-start.3
  199.5 5.7 %copy-start.10 = (f32[224,1024]{1,0:T(8,128)}, f32[224,1024]{1,0:T(8,128)S(1)}, u32[]{:S(2)}) copy-start(f32[224,1024]{1,0:T(8,128)S(1)} %get-tuple-element.100) | copy-start | bytes 2752516
  199.6 27.0 %slice-start.7 = ((s8[8650752]{0:T(1024)(128)(4,1)}), s8[4194304]{0:T(1024)(128)(4,1)S(1)}, s32[]{:S(2)}) async-start(s8[8650752]{0:T(1024)(128)(4,1)} %bitcast.142), calls=%async_computation.7 | async-start | bytes 8388608
  205.3 21.3 %slice-start.8 = ((s8[8650752]{0:T(1024)(128)(4,1)}), s8[4194304]{0:T(1024)(128)(4,1)S(1)}, s32[]{:S(2)}) async-start(s8[8650752]{0:T(1024)(128)(4,1)} %bitcast.142), calls=%async_computation.8 | async-start | bytes 8388608
  205.6 3.5 %copy-start.4 = (bf16[2,4,2,128,1024]{4,3,2,1,0:T(8,128)(2,1)S(1)}, bf16[2,4,2,128,1024]{4,3,2,1,0:T(8,128)(2,1)}, u32[]{:S(2)}) copy-start(bf16[2,4,2,128,1024]{4,3,2,1,0:T(8,128)(2,1)} %get-tuple-element.26) | copy-start | bytes 12582916
  209.0 17.5 %slice-start.9 = ((s8[8650752]{0:T(1024)(128)(4,1)}), s8[262144]{0:T(1024)(128)(4,1)S(1)}, s32[]{:S(2)}) async-start(s8[8650752]{0:T(1024)(128)(4,1)} %bitcast.142), calls=%async_computation.9 | async-start | bytes 524288
  237.8 94.0 %copy-start.11 = (f32[224,1024]{1,0:T(8,128)S(1)}, f32[224,1024]{1,0:T(8,128)}, u32[]{:S(2)}) copy-start(f32[224,1024]{1,0:T(8,128)} %copy-done.10) | copy-start | bytes 2752516
  331.8 3.8 %copy-start.15 = (f32[128,1024]{1,0:T(8,128)S(1)}, f32[128,1024]{1,0:T(8,128)}, u32[]{:S(2)}) copy-start(f32[128,1024]{1,0:T(8,128)} %get-tuple-element.38) | copy-start | bytes 1572868
  331.8 4.5 %copy-start.13 = (f32[64,4096]{1,0:T(8,128)S(1)}, f32[64,4096]{1,0:T(8,128)}, u32[]{:S(2)}) copy-start(f32[64,4096]{1,0:T(8,128)} %get-tuple-element.39) | copy-start | bytes 3145732
  (7 other events, 16.2 us)
where the time goes:
time: 344 us; the launch traced here: 338 us
  Pallas kernels  211 us (61%)
  matrix products  70.8 us (21%)
  waiting for transfers between devices  23.3 us (7%)
  local copies, waits for them, and re-layouts  15.5 us (5%)
  other arithmetic  9.79 us (3%)
  starting transfers between devices  6.28 us (2%)
    pallas_call x1, Pallas kernels, scatter_sums(): pl.pallas_call(scatter_kernel, in_specs=[pl.BlockSpec(memory_space=pl.ANY...  89.8 us
    pallas_call x1, Pallas kernels, gather_shards(): pl.pallas_call(gather_kernel, in_specs=[pl.BlockSpec(memory_space=pl.ANY)...  78 us
    pallas_call x2, Pallas kernels, mix_backward(): pl.pallas_call(mix_backward_kernel, grid=(blocks,), in_specs=[per_block((...  31.1 us
    dot_general x8, matrix products, back_product(): lax.dot_general(grad_rows, weight, (((1,), (1,)), ((), ())), preferred_el...  27.5 us
    dot_general x8, matrix products, forward_product(): return jnp.dot(left, weight, preferred_element_type=F32)  25.1 us
    ppermute x2, waiting for transfers between devices, across(): return lax.ppermute(array, 'section', [(0, 1)] if by > 0 else [(1, 0)])  23.3 us
    dot_general x4, matrix products, outer_sum(): lax.dot_general(left, right, (((0,), (0,)), ((), ())), preferred_element_...  18.3 us
    pallas_call x2, Pallas kernels, mix_forward(): pl.pallas_call(mix_forward_kernel, grid=(blocks,), in_specs=[per_block((T...  12.2 us
  transfers between devices with their start and end apart: 2, of which 2 were waited for; matrix products, arithmetic and copies ran while one was open for 0% of the time, Pallas kernels for 0%

commit v1 on v0

--- a/solution.py
+++ b/solution.py
@@ -90,9 +90,17 @@
     return raw, dt, decay, exact_dot(lower, decay)
 
 
-def attention_probs(q_tile, keep, k_dup, allowed):
-    scores = dot_nt(jnp.where(keep, q_tile, 0.0), k_dup) * (1.0 / math.sqrt(HEAD_WIDTH))
-    scores = jnp.where(allowed, scores, -1e30)
+def stacked(tile, left):
+    return jnp.concatenate([jnp.where(left, tile, 0.0), jnp.where(left, 0.0, tile)], 0).astype(BF16)
+
+
+def picked(tiles, left):
+    return jnp.where(left, tiles[:T], tiles[T:])
+
+
+def attention_probs(q_stack, k_dup, both_allowed):
+    scores = dot_nt(q_stack, k_dup) * (1.0 / math.sqrt(HEAD_WIDTH))
+    scores = jnp.where(both_allowed, scores, -1e30)
     e = jnp.exp(scores - jnp.max(scores, -1, keepdims=True))
     return e / jnp.sum(e, -1, keepdims=True)
 
@@ -112,22 +120,26 @@
     for pair in range(MHEADS // 2):
         sl = slice(128 * pair, 128 * pair + 128)
         xs = act_ref[:, sl]
-        ys = []
+        parts = []
         for h in (2 * pair, 2 * pair + 1):
             decayed = jnp.exp(jnp.where(allowed, cum[:, h : h + 1] - cum_t[h : h + 1, :], -1e30))
-            ys.append(dot_nn(decayed * cb * dt_t[h : h + 1, :], xs))
-        y = jnp.where(left, ys[0], ys[1]) + skip_ref[0:1, sl] * xs
+            parts.append((decayed * cb * dt_t[h : h + 1, :]).astype(BF16))
+        y = picked(dot_nn(jnp.concatenate(parts, 0), xs), left) + skip_ref[0:1, sl] * xs
         z = p_ref[0, :, sl]
         u_ref[0, :, sl] = (y * (z * jax.nn.sigmoid(z))).astype(BF16)
-    k_dups = doubled(p_ref[0, :, OFF_K:OFF_V], left)
-    v_dups = doubled(p_ref[0, :, OFF_V:OFF_R], left)
+    k_dups = [tile.astype(BF16) for tile in doubled(p_ref[0, :, OFF_K:OFF_V], left)]
+    v_dups = [tile.astype(BF16) for tile in doubled(p_ref[0, :, OFF_V:OFF_R], left)]
+    places = iota((2 * T, T), 0)
+    marks = jnp.concatenate([segc_ref[0], segc_ref[0]], 0)[:, :T]
+    both_allowed = (marks == segr_ref[0][0:1, :]) & (
+        jnp.where(places >= T, places - T, places) >= iota((2 * T, T), 1)
+    )
     for pair in range(QUERY_HEAD_COUNT // 2):
         kv = pair // 2
         q_tile = p_ref[0, :, OFF_Q + 128 * pair : OFF_Q + 128 * pair + 128]
-        probs = [attention_probs(q_tile, keep, k_dups[kv], allowed) for keep in (left, ~left)]
-        out = [dot_nn(pr, v_dups[kv]) for pr in probs]
-        u_ref[0, :, SSM + 128 * pair : SSM + 128 * pair + 128] = jnp.where(
-            left, out[0], out[1]
+        probs = attention_probs(stacked(q_tile, left), k_dups[kv], both_allowed)
+        u_ref[0, :, SSM + 128 * pair : SSM + 128 * pair + 128] = picked(
+            dot_nn(probs, v_dups[kv]), left
         ).astype(BF16)
 
 
@@ -156,24 +168,24 @@
         gm = gu_ref[0, :, sl]
         sg = jax.nn.sigmoid(z)
         gy = gm * (z * sg)
-        gy16 = gy.astype(BF16)
-        ys, gxs = [], []
-        for h, keep in ((2 * pair, left), (2 * pair + 1, ~left)):
+        gy_stack = stacked(gy, left)
+        gks = dot_nt(gy_stack, xs16)
+        parts = []
+        for side, h in enumerate((2 * pair, 2 * pair + 1)):
             decayed = jnp.exp(jnp.where(allowed, cum[:, h : h + 1] - cum_t[h : h + 1, :], -1e30))
             dt_row = dt_t[h : h + 1, :]
             base = decayed * cb
-            k16 = (base * dt_row).astype(BF16)
-            ys.append(dot_nn(k16, xs16))
-            gxs.append(dot_tn(k16, gy16))
-            gk = dot_nt(jnp.where(keep, gy, 0.0), xs16)
+            parts.append((base * dt_row).astype(BF16))
+            gk = gks[side * T : side * T + T]
             gcb = gcb + gk * (decayed * dt_row)
             q = gk * base
             colq_ref[h : h + 1, :] = jnp.sum(q, 0, keepdims=True)
             row_form = jnp.where(lanes == h, jnp.sum(q * dt_row, 1, keepdims=True), row_form)
         skip = skip_ref[0:1, sl]
-        y = jnp.where(left, ys[0], ys[1]) + skip * xs
+        kernels = jnp.concatenate(parts, 0)
+        y = picked(dot_nn(kernels, xs16), left) + skip * xs
         gp_ref[0, :, sl] = (gm * y * (sg * (1.0 + z * (1.0 - sg)))).astype(BF16)
-        gact_ref[:, sl] = jnp.where(left, gxs[0], gxs[1]) + skip * gy
+        gact_ref[:, sl] = dot_tn(kernels, gy_stack) + skip * gy
         gskip_ref[0, 0:1, sl] = jnp.sum(gy * xs, 0, keepdims=True)
     gact_ref[:, SSM : SSM + STATE] = dot_tn(gcb, c_rows)
     gact_ref[:, SSM + STATE :] = dot_nn(gcb, b_rows)
@@ -199,9 +211,15 @@
             gc = gc + pltpu.roll(linked, T - j, 0) * conv_ref[j : j + 1, sl]
             gconv_ref[0, j : j + 1, sl] = jnp.sum(linked * pltpu.roll(c, j, 0), 0, keepdims=True)
         gconv_ref[0, 4:5, sl] = jnp.sum(gmix, 0, keepdims=True)
+        gconv_ref[0, 5:8, sl] = jnp.zeros((3, 128), F32)
         gp_ref[0, :, SSM + at : SSM + at + 128] = gc.astype(BF16)
-    k_dups = doubled(p_ref[0, :, OFF_K:OFF_V], left)
-    v_dups = doubled(p_ref[0, :, OFF_V:OFF_R], left)
+    k_dups = [tile.astype(BF16) for tile in doubled(p_ref[0, :, OFF_K:OFF_V], left)]
+    v_dups = [tile.astype(BF16) for tile in doubled(p_ref[0, :, OFF_V:OFF_R], left)]
+    places = iota((2 * T, T), 0)
+    marks = jnp.concatenate([segc_ref[0], segc_ref[0]], 0)[:, :T]
+    both_allowed = (marks == segr_ref[0][0:1, :]) & (
+        jnp.where(places >= T, places - T, places) >= iota((2 * T, T), 1)
+    )
     gks, gvs = [], []
     for kv in range(KVHEADS):
         gk_sum = jnp.zeros((T, 128), F32)
@@ -210,18 +228,14 @@
             sl = slice(OFF_Q + 128 * pair, OFF_Q + 128 * pair + 128)
             q_tile = p_ref[0, :, sl]
             go = gu_ref[0, :, SSM + 128 * pair : SSM + 128 * pair + 128]
-            gq, gk, gv = [], [], []
-            for keep in (left, ~left):
-                probs = attention_probs(q_tile, keep, k_dups[kv], allowed)
-                gpr = dot_nt(jnp.where(keep, go, 0.0), v_dups[kv])
-                gs = probs * (gpr - jnp.sum(gpr * probs, -1, keepdims=True))
-                gs = (gs * (1.0 / math.sqrt(HEAD_WIDTH))).astype(BF16)
-                gq.append(dot_nn(gs, k_dups[kv]))
-                gk.append(dot_tn(gs, q_tile))
-                gv.append(dot_tn(probs, go))
-            gp_ref[0, :, sl] = jnp.where(left, gq[0], gq[1]).astype(BF16)
-            gk_sum = gk_sum + jnp.where(left, gk[0], gk[1])
-            gv_sum = gv_sum + jnp.where(left, gv[0], gv[1])
+            q_stack, go_stack = stacked(q_tile, left), stacked(go, left)
+            probs = attention_probs(q_stack, k_dups[kv], both_allowed)
+            gpr = dot_nt(go_stack, v_dups[kv])
+            gs = probs * (gpr - jnp.sum(gpr * probs, -1, keepdims=True))
+            gs = (gs * (1.0 / math.sqrt(HEAD_WIDTH))).astype(BF16)
+            gp_ref[0, :, sl] = picked(dot_nn(gs, k_dups[kv]), left).astype(BF16)
+            gk_sum = gk_sum + dot_tn(gs, q_stack)
+            gv_sum = gv_sum + dot_tn(probs, go_stack)
         gks.append(gk_sum + pltpu.roll(gk_sum, HEAD_WIDTH, 1))
         gvs.append(gv_sum + pltpu.roll(gv_sum, HEAD_WIDTH, 1))
     gp_ref[0, :, OFF_K:OFF_V] = jnp.where(left, gks[0], gks[1]).astype(BF16)
@@ -429,9 +443,9 @@
 
 
 def scatter_kernel(*refs):
-    grads, extra, outs, smalls = refs[:4], refs[4], refs[5:9], refs[9:12]
-    accs, wholes, cores = refs[12:16], refs[16:20], refs[20 : 20 + len(SCATTERED)]
-    arrivals = refs[20 + len(SCATTERED) : -7]
+    grads, extra, wholes, smalls = refs[:4], refs[4], refs[5:9], refs[9:12]
+    accs, cores = refs[12:16], refs[16 : 16 + len(SCATTERED)]
+    arrivals = refs[16 + len(SCATTERED) : -7]
     local_sem, core_send, core_recv, send_sem, recv_sem, last_send, last_recv = refs[-7:]
     section, y, z, core, x = place()
     near = neighbours(section, y, z, core, x)
@@ -508,16 +522,14 @@
             copy.start()
             last.append(copy)
         wholes[array][mine, :] = accs[array][y, z, mine, :]
-    for array in range(4):
-        for k in range(3):
-            last[array * 3 + k].wait_recv()
-        outs[array][...] = wholes[array][:, : outs[array].shape[1]].astype(F32)
+    for copy in last:
+        copy.wait_recv()
     small = wholes[0][:, EXTRA:].astype(F32)
     out_gains, out_conv, out_head = smalls
-    out_gains[...] = small[:, :2]
-    out_conv[:56, :] = small[:56, 2 : 3 + CONV]
-    out_conv[56:, :] = small[:56, 3 + CONV : 4 + 2 * CONV]
-    out_head[...] = small[:MHEADS, 12:15]
+    out_conv[:, :56] = small[: CONV + 1, :56]
+    out_conv[:, 56:] = small[8 : 9 + CONV, :56]
+    out_gains[...] = small[16:18, :64]
+    out_head[...] = small[24:27, :MHEADS]
     for copy in last + swaps + [c for copies in flying.values() for c in copies]:
         copy.wait_send()
 
@@ -526,16 +538,16 @@
     n_copies = sum(shape[0] for shape in stage_shapes(SCATTERED))
     n_parts = len(SCATTERED)
     out_shapes = [
-        (64, PIN), (128, 1024), (64, 2 * FF), (128, 1024), (64, 2), (112, CONV + 1), (MHEADS, 3),
+        *[jax.ShapeDtypeStruct(s, BF16) for s in zip(SHARD_ROWS, SUM_COLS)],
+        *[jax.ShapeDtypeStruct(s, F32) for s in ((2, 64), (CONV + 1, T), (3, MHEADS))],
     ]
     return pl.pallas_call(
         scatter_kernel,
         in_specs=[pl.BlockSpec(memory_space=pl.ANY)] * 5,
         out_specs=[pl.BlockSpec(memory_space=pltpu.VMEM)] * 7,
-        out_shape=[jax.ShapeDtypeStruct(s, F32) for s in out_shapes],
+        out_shape=out_shapes,
         scratch_shapes=[
             *[pltpu.VMEM((2, 4, r, c), BF16) for r, c in zip(SHARD_ROWS, SUM_COLS)],
-            *[pltpu.VMEM((r, c), BF16) for r, c in zip(SHARD_ROWS, SUM_COLS)],
             *[pltpu.VMEM((2, 4, SHARD_ROWS[a], cols), BF16) for a, _, cols, _ in SCATTERED],
             *[pltpu.VMEM(shape, BF16) for shape in stage_shapes(SCATTERED)],
             pltpu.SemaphoreType.DMA((n_parts,)),
@@ -729,26 +741,28 @@
     return lax.ppermute(array, "section", [(0, 1)] if by > 0 else [(1, 0)])
 
 
-def split_conv(table):
-    parts = table.reshape(-1, 2, 56, CONV + 1).transpose(0, 2, 1, 3).reshape(-1, 56, 2 * (CONV + 1))
-    return jnp.pad(parts, ((0, 0), (0, 8), (0, 0))).reshape(-1, 2 * (CONV + 1))
-
-
-def join_conv(parts):
-    parts = parts[:, :56].reshape(-1, 56, 2, CONV + 1)
-    return parts.transpose(3, 0, 2, 1).reshape(CONV + 1, -1)
-
-
 def gather_weights(norm_gains, w_in, conv_params, w_out, w_gate_up, w_down):
-    filler = jnp.zeros((w_in.shape[0], PAD - PIN - 12), BF16)
-    tail = jnp.concatenate([w_in[:, TAIL:], norm_gains, split_conv(conv_params), filler], 1)
+    rows = w_in.shape[0]
+    conv_rows = conv_params.T
+    small = jnp.concatenate(
+        [
+            jnp.pad(conv_rows[:, :56], ((0, 3), (0, 8))),
+            jnp.pad(conv_rows[:, 56:], ((0, 3), (0, 8))),
+            norm_gains.T,
+        ],
+        0,
+    )
+    small = jnp.pad(small, ((0, rows - small.shape[0]), (0, PAD - PIN - 64)))
+    tail = jnp.concatenate([w_in[:, TAIL:], small], 1)
     parts = gather_shards(
         [a.reshape(1, 1, 1, *a.shape) for a in (w_in, w_out, w_gate_up, w_down)],
         tail.reshape(1, 1, 1, *tail.shape),
     )
-    small = parts[0][..., PIN : PIN + 12].reshape(16, 64, 12).astype(F32)
-    gains = small[:, :, :2].reshape(-1, 2).T
-    return (gains, *[a.reshape(-1, a.shape[-1]) for a in parts]), join_conv(small[:, :, 2:])
+    small = parts[0][..., PIN : PIN + 64].reshape(-1, rows, 64)[:, :18].astype(F32)
+    gains = small[:, 16:18].transpose(1, 0, 2).reshape(2, -1)
+    conv_rows = small[:, :16, :56].reshape(-1, 2, 8, 56)[:, :, : CONV + 1]
+    conv_rows = conv_rows.transpose(2, 0, 1, 3).reshape(CONV + 1, -1)
+    return (gains, *[a.reshape(-1, a.shape[-1]) for a in parts]), conv_rows
 
 
 def body(
@@ -786,14 +800,20 @@
     grad_gain_one, grad_gain_two, grad_conv, grad_head, grad_skip = smalls
     sums = [outer_sum(left, right) for left, right in pairs]
     shards = lax.axis_size("shard")
-    gains = jnp.stack([grad_gain_one, grad_gain_two], 1)
-    conv = split_conv(jnp.sum(grad_conv, 0)[: CONV + 1].T)
-    head = jnp.sum(grad_head, 0)[:2, :MHEADS]
+    gains = jnp.stack([grad_gain_one, grad_gain_two]).reshape(2, shards, 64).transpose(1, 0, 2)
+    conv = jnp.sum(grad_conv, 0).reshape(8, shards, 2, 56).transpose(1, 2, 0, 3)
+    conv = conv.reshape(shards, 16, 56)
     skip = jnp.sum(jnp.sum(grad_skip, 0)[0].reshape(MHEADS, HEAD_WIDTH), 1)
-    head = jnp.pad(jnp.concatenate([head, skip[None]], 0).T, ((0, 64 - MHEADS), (0, 0)))
-    head = jnp.broadcast_to(head[None], (shards, 64, 3)).reshape(shards * 64, 3)
-    extra = jnp.concatenate([gains, conv, head], 1)
-    extra = jnp.pad(extra, ((0, 0), (0, 128 - extra.shape[1]))).astype(BF16)
+    head = jnp.concatenate([jnp.sum(grad_head, 0)[:2, :MHEADS], skip[None]], 0)
+    head = jnp.broadcast_to(head[None], (shards, 3, MHEADS))
+    extra = jnp.concatenate(
+        [
+            jnp.pad(conv, ((0, 0), (0, 0), (0, 72))),
+            jnp.pad(gains, ((0, 0), (0, 6), (0, 64))),
+            jnp.pad(head, ((0, 0), (0, 37), (0, 128 - MHEADS))),
+        ],
+        1,
+    ).astype(BF16)
     out_in, out_out, out_gu, out_dn, out_gains, out_conv, out_head = scatter_sums(
         [g.reshape(2, 4, 2, g.shape[0] // 16, g.shape[1]) for g in sums],
         extra.reshape(2, 4, 2, 64, 128),
@@ -801,13 +821,13 @@
     return (
         result.astype(BF16).reshape(1, blocks, T, width),
         grad_input.reshape(1, blocks, T, width),
-        out_gains[None],
-        out_in[None],
-        out_conv[None],
-        out_head[None],
-        out_out[None],
-        out_gu[None],
-        out_dn[None],
+        out_gains.T[None],
+        out_in[None, :, :PIN].astype(F32),
+        out_conv.T[None],
+        out_head.T[None],
+        out_out[None].astype(F32),
+        out_gu[None].astype(F32),
+        out_dn[None].astype(F32),
     )
 
 

time: 344 us -> 330 us (0.959)
  Pallas kernels: 211 us -> 199 us
  local copies, waits for them, and re-layouts: 15.5 us -> 8.76 us
  other arithmetic: 9.79 us -> 15.1 us
    pallas_call x2, Pallas kernels: 31.1 us -> 22.8 us  [mix_backward(): pl.pallas_call(mix_backward_kernel, grid=(blocks,), in_specs=[per_block((...]
    convert_element_type x1 -> x4, other arithmetic: 0.06 us -> 5.33 us  [the longest x1 2.14 us: body(): out_gu[None].astype(F32)]
    unnamed x66 -> x62, local copies, waits for them, and re-layouts: 8.52 us -> 4.98 us
where the time goes in v1:
time: 330 us; the launch traced here: 325 us
  Pallas kernels  199 us (60%)
  matrix products  70.7 us (21%)
  waiting for transfers between devices  23.3 us (7%)
  other arithmetic  15.1 us (5%)
  local copies, waits for them, and re-layouts  8.76 us (3%)
  starting transfers between devices  6.3 us (2%)
    pallas_call x1, Pallas kernels, scatter_sums(): pl.pallas_call(scatter_kernel, in_specs=[pl.BlockSpec(memory_space=pl.ANY...  89 us
    pallas_call x1, Pallas kernels, gather_shards(): pl.pallas_call(gather_kernel, in_specs=[pl.BlockSpec(memory_space=pl.ANY)...  78 us
    dot_general x8, matrix products, back_product(): lax.dot_general(grad_rows, weight, (((1,), (1,)), ((), ())), preferred_el...  27.5 us
    dot_general x8, matrix products, forward_product(): return jnp.dot(left, weight, preferred_element_type=F32)  25 us
    ppermute x2, waiting for transfers between devices, across(): return lax.ppermute(array, 'section', [(0, 1)] if by > 0 else [(1, 0)])  23.3 us
    pallas_call x2, Pallas kernels, mix_backward(): pl.pallas_call(mix_backward_kernel, grid=(blocks,), in_specs=[per_block((...  22.8 us
    dot_general x4, matrix products, outer_sum(): lax.dot_general(left, right, (((0,), (0,)), ((), ())), preferred_element_...  18.2 us
    pallas_call x2, Pallas kernels, mix_forward(): pl.pallas_call(mix_forward_kernel, grid=(blocks,), in_specs=[per_block((T...  9.33 us
  transfers between devices with their start and end apart: 2, of which 2 were waited for; matrix products, arithmetic and copies ran while one was open for 0% of the time, Pallas kernels for 0%

profile of v1, /device:TPU:1, one launch (start us, length us, event | category | flops | bytes accessed | tf_op | source)
XLA Modules:
  0.0 324.8 jit_solution(11172976130456848734)
XLA Ops:
  3.6 78.0 %gather_shards.1 = (bf16[2,4,2,64,4224]{4,3,2,1,0:T(8,128)(2,1)}, bf16[2,4,2,128,1024]{4,3,2,1,0:T(8,128)(2,1)}, bf16[2,4,2,64,4096]{4,3,2,1,0:T(8,128)(2,1)}, bf16[2,4,2,128,1024]{4,3,2,1,0:T(8,128)(2,1)}) custom-call(bf16[1,1,1,64,4120]{4,3,2,1,0:T(8,128)(2,1)} %bitcast.161, bf16[1,1,1,128,1024]{4,3,2,1,0:T(8,128)(2,1)} %bitcast.164, ...), custom_call_target="tpu_custom_call" | custom-call | tf_op jit(solution)/shard_map/gather_shards/pallas_call | solution.py:649
  85.9 5.7 %fusion.35.p_ref = f32[2,112,4224]{2,1,0:T(8,128)S(1)} fusion(bf16[1024,4224,1]{1,0,2:T(8,128)(2,1)} %bitcast.138, bf16[2,112,1024]{2,1,0:T(8,128)(2,1)S(1)} %copy-done.6, f32[1024]{0:T(1024)S(1)} %mul.119, f32[2,112]{1,0:T(2,128)S(1)} %add_rsqrt_fusion.3), kind=kOutput, calls=%fused_computation.66 | convolution fusion | flops 1938685952 | bytes 12899200 | tf_op jit(solution)/shard_map/dot_general | solution.py:681
  91.8 4.6 %mix_forward.2 = bf16[2,112,2048]{2,1,0:T(8,128)(2,1)S(1)} custom-call(f32[2,112,4224]{2,1,0:T(8,128)S(1)} %fusion.35.p_ref, f32[2,112,128]{2,1,0:T(8,128)S(1)} %broadcast_in_dim.18.segc_ref, f32[2,8,112]{2,1,0:T(8,128)S(1)} %broadcast_in_dim.19.segr_ref, f32[8,1792]{1,0:T(8,128)S(1)} %pad.38.conv_ref, f32[8,128]{1,0:T(8,128)S(1)} %pad.39.head_ref, ...), custom_call_target="tpu_custom_call" | custom-call | tf_op jit(solution)/shard_map/mix_forward/pallas_call | solution.py:261
  97.6 5.7 %fusion.34 = f32[224,4096]{1,0:T(8,128)S(1)} fusion(bf16[1024,4096]{1,0:T(8,128)(2,1)} %bitcast.129, f32[224,1024]{1,0:T(8,128)S(1)} %get-tuple-element.95, f32[1024]{0:T(1024)S(1)} %mul.125, f32[224]{0:T(256)S(1)} %add_rsqrt_fusion.2), kind=kOutput, calls=%fused_computation.65 | convolution fusion | flops 1879736320 | bytes 12981120 | tf_op jit(solution)/shard_map/dot_general | solution.py:681
  104.6 4.8 %collective-permute-start = (bf16[224,1024]{1,0:T(8,128)(2,1)S(1)}, bf16[224,1024]{1,0:T(8,128)(2,1)S(1)}, u32[]{:S(2)}, u32[]{:S(2)}) collective-permute-start(bf16[224,1024]{1,0:T(8,128)(2,1)S(1)} %fusion.15), channel_id=1, source_target_pairs={{0,64},{1,65},{2,66},{3,67},{4,68},{5,69},{6,70},{7,71},{8,72},{9,... | collective-permute-start | bytes 1376264 | tf_op jit(solution)/shard_map/ppermute | solution.py:741
  109.5 9.7 %collective-permute-done = bf16[224,1024]{1,0:T(8,128)(2,1)S(1)} collective-permute-done((bf16[224,1024]{1,0:T(8,128)(2,1)S(1)}, bf16[224,1024]{1,0:T(8,128)(2,1)S(1)}, u32[]{:S(2)}, u32[]{:S(2)}) %collective-permute-start) | collective-permute-done | bytes 458784 | tf_op jit(solution)/shard_map/ppermute | solution.py:741
  119.6 5.8 %fusion.59.p_ref = f32[2,112,4224]{2,1,0:T(8,128)S(1)} fusion(bf16[2,112,1024]{2,1,0:T(8,128)(2,1)S(1)} %bitcast.153, bf16[1024,4224,1]{1,0,2:T(8,128)(2,1)} %bitcast.139), kind=kOutput, calls=%fused_computation.120 | convolution fusion | flops 1937768448 | bytes 12894208 | tf_op jit(solution)/shard_map/dot_general | solution.py:681
  125.5 4.7 %mix_forward.3 = bf16[2,112,2048]{2,1,0:T(8,128)(2,1)S(1)} custom-call(f32[2,112,4224]{2,1,0:T(8,128)S(1)} %fusion.59.p_ref, f32[2,112,128]{2,1,0:T(8,128)S(1)} %broadcast_in_dim.18.segc_ref, f32[2,8,112]{2,1,0:T(8,128)S(1)} %broadcast_in_dim.19.segr_ref, f32[8,1792]{1,0:T(8,128)S(1)} %pad.38.conv_ref, f32[8,128]{1,0:T(8,128)S(1)} %pad.39.head_ref, ...), custom_call_target="tpu_custom_call" | custom-call | tf_op jit(solution)/shard_map/mix_forward/pallas_call | solution.py:261
  131.5 2.2 fusion.55
  133.8 3.2 multiply_convert_fusion.3
  137.1 4.4 %multiply_reduce_fusion.2 = (f32[224]{0:T(256)S(1)}, f32[224,1024]{1,0:T(8,128)S(1)}) fusion(f32[224,1024]{1,0:T(8,128)S(1)} %get-tuple-element.97, f32[224]{0:T(256)S(1)} %add_rsqrt_fusion, f32[1024]{0:T(1024)S(1)} %mul.125, bf16[1024,4096]{1,0:T(8,128)(2,1)S(1)} %bitcast.133, bf16[224,2048]{1,0:T(8,128)(2,1)} %get-tuple-element.88, ...), kind=kOutput, calls=%fused_computation.58 | convolution fusion | flops 1883635456 | bytes 12064512 | tf_op jit(solution)/shard_map/dot_general | solution.py:685
  142.5 3.7 %fusion.60.gu_ref = f32[2,112,2048]{2,1,0:T(8,128)S(1)} fusion(bf16[2,112,1024]{2,1,0:T(8,128)(2,1)S(1)} %bitcast.158, bf16[2048,1024,1]{1,0,2:T(8,128)(2,1)} %bitcast.149), kind=kOutput, calls=%fused_computation.121 | convolution fusion | flops 939524096 | bytes 6488064 | tf_op jit(solution)/shard_map/dot_general | solution.py:685
  146.2 11.8 %mix_backward.2 = (bf16[2,112,4224]{2,1,0:T(8,128)(2,1)S(1)}, f32[2,8,1792]{2,1,0:T(8,128)}, f32[2,8,128]{2,1,0:T(8,128)}, f32[2,8,1536]{2,1,0:T(8,128)}) custom-call(f32[2,112,4224]{2,1,0:T(8,128)S(1)} %fusion.59.p_ref, f32[2,112,2048]{2,1,0:T(8,128)S(1)} %fusion.60.gu_ref, f32[2,112,128]{2,1,0:T(8,128)S(1)} %broadcast_in_dim.18.segc_ref, ...), custom_call_target="tpu_custom_call" | custom-call | tf_op jit(solution)/shard_map/mix_backward/pallas_call | solution.py:275
  158.1 2.8 fusion.22
  163.6 13.6 %collective-permute-done.1 = bf16[224,1024]{1,0:T(8,128)(2,1)} collective-permute-done((bf16[224,1024]{1,0:T(8,128)(2,1)}, bf16[224,1024]{1,0:T(8,128)(2,1)}, u32[]{:S(2)}, u32[]{:S(2)}) %collective-permute-start.1) | collective-permute-done | bytes 458784 | tf_op jit(solution)/shard_map/ppermute | solution.py:741
  178.4 5.3 %multiply_convert_fusion.1 = (bf16[224,2048]{1,0:T(8,128)(2,1)S(1)}, bf16[224,2048]{1,0:T(8,128)(2,1)S(1)}, bf16[224,2048]{1,0:T(8,128)(2,1)S(1)}) fusion(f32[224,4096]{1,0:T(8,128)} %copy-done.7, bf16[224,1024]{1,0:T(8,128)(2,1)S(1)} %broadcast_select_fusion, bf16[2048,1024]{1,0:T(8,128)(2,1)} %bitcast.178), kind=kOutput, calls=%fused_computation.13 | convolution fusion | flops 946405376 | bytes 11075584 | tf_op jit(solution)/shard_map/dot_general | solution.py:685
  185.7 3.2 convolution_convert_fusion.2
  188.9 2.9 multiply_reduce_fusion
  191.8 5.7 %convolution_convert_fusion.1 = bf16[1024,4096]{1,0:T(8,128)(2,1)} fusion(bf16[224,2048]{1,0:T(8,128)(2,1)S(1)} %get-tuple-element.86, bf16[224,2048]{1,0:T(8,128)(2,1)S(1)} %get-tuple-element.85, f32[224,1024]{1,0:T(8,128)S(1)} %get-tuple-element.97, f32[224]{0:T(256)S(1)} %add_rsqrt_fusion, f32[1024]{0:T(1024)S(1)} %mul.125), kind=kOutput, calls=%fused_computation.1 | convolution fusion | flops 1887600640 | bytes 11146112 | tf_op jit(solution)/shard_map/dot_general | solution.py:691
  197.8 3.5 %convolution_convert_fusion.3 = bf16[2048,1024]{1,0:T(8,128)(2,1)} fusion(bf16[224,2048]{1,0:T(8,128)(2,1)S(1)} %bitcast.124, bf16[224,1024]{1,0:T(8,128)(2,1)S(1)} %fusion.57), kind=kOutput, calls=%fused_computation.3 | convolution fusion | flops 941621248 | bytes 5570560 | tf_op jit(solution)/shard_map/dot_general | solution.py:691
  203.6 10.9 %mix_backward.3 = (bf16[2,112,4224]{2,1,0:T(8,128)(2,1)S(1)}, f32[2,8,1792]{2,1,0:T(8,128)S(1)}, f32[2,8,128]{2,1,0:T(8,128)S(1)}, f32[2,8,1536]{2,1,0:T(8,128)S(1)}) custom-call(f32[2,112,4224]{2,1,0:T(8,128)S(1)} %copy-done.1, f32[2,112,2048]{2,1,0:T(8,128)S(1)} %fusion.61.gu_ref, f32[2,112,128]{2,1,0:T(8,128)S(1)} %broadcast_in_dim.18.segc_ref, ...), custom_call_target="tpu_custom_call" | custom-call | tf_op jit(solution)/shard_map/mix_backward/pallas_call | solution.py:275
  214.6 3.6 %fusion.31 = (bf16[1024]{0:T(1024)(128)(2,1)S(1)}, f32[224]{0:T(256)S(1)}, f32[224,1024]{1,0:T(8,128)}) fusion(bf16[224,1024]{1,0:T(8,128)(2,1)S(1)} %get-tuple-element.84, f32[224]{0:T(256)S(1)} %add_rsqrt_fusion.1, f32[1024]{0:T(1024)S(1)} %mul.119, bf16[224,4224]{1,0:T(8,128)(2,1)S(1)} %bitcast.125, bf16[1024,4224]{1,0:T(8,128)(2,1)S(1)} %bitcast.145), kind=kOutput, calls=%fused_computation.52 | convolution fusion | flops 1939372800 | bytes 11927296 | tf_op jit(solution)/shard_map/dot_general | solution.py:685
  218.2 5.9 %convolution_convert_fusion = bf16[1024,4224]{1,0:T(8,128)(2,1)} fusion(bf16[224,1024]{1,0:T(8,128)(2,1)S(1)} %fusion.21, bf16[224,4224]{1,0:T(8,128)(2,1)S(1)} %bitcast.126), kind=kOutput, calls=%fused_computation | convolution fusion | flops 1942093824 | bytes 11001856 | tf_op jit(solution)/shard_map/dot_general | solution.py:691
  225.6 89.0 %scatter_sums.1 = (bf16[64,4352]{1,0:T(8,128)(2,1)}, bf16[128,1024]{1,0:T(8,128)(2,1)}, bf16[64,4096]{1,0:T(8,128)(2,1)}, bf16[128,1024]{1,0:T(8,128)(2,1)}, f32...) custom-call(bf16[2,4,2,64,4224]{4,3,2,1,0:T(8,128)(2,1)} %bitcast.137, bf16[2,4,2,128,1024]{4,3,2,1,0:T(8,128)(2,1)} %bitcast.148, ...), custom_call_target="tpu_custom_call" | custom-call | tf_op jit(solution)/shard_map/scatter_sums/pallas_call | solution.py:544
  (132 shorter events, 32.4 us)
Async XLA Ops:
  0.6 85.3 %copy-start.6 = (bf16[2,112,1024]{2,1,0:T(8,128)(2,1)S(1)}, bf16[2,112,1024]{2,1,0:T(8,128)(2,1)}, u32[]{:S(2)}) copy-start(bf16[2,112,1024]{2,1,0:T(8,128)(2,1)} %param.10) | copy-start | bytes 1376260
  91.6 4.8 %copy-start.2 = (bf16[2,4,2,128,1024]{4,3,2,1,0:T(8,128)(2,1)S(1)}, bf16[2,4,2,128,1024]{4,3,2,1,0:T(8,128)(2,1)}, u32[]{:S(2)}) copy-start(bf16[2,4,2,128,1024]{4,3,2,1,0:T(8,128)(2,1)} %get-tuple-element.26) | copy-start | bytes 12582916
  97.6 5.7 %copy-start.16 = (bf16[2,4,2,128,1024]{4,3,2,1,0:T(8,128)(2,1)S(1)}, bf16[2,4,2,128,1024]{4,3,2,1,0:T(8,128)(2,1)}, u32[]{:S(2)}) copy-start(bf16[2,4,2,128,1024]{4,3,2,1,0:T(8,128)(2,1)} %get-tuple-element.28) | copy-start | bytes 12582916
  104.6 14.6 %collective-permute-start = (bf16[224,1024]{1,0:T(8,128)(2,1)S(1)}, bf16[224,1024]{1,0:T(8,128)(2,1)S(1)}, u32[]{:S(2)}, u32[]{:S(2)}) collective-permute-start(bf16[224,1024]{1,0:T(8,128)(2,1)S(1)} %fusion.15), channel_id=1, source_target_pairs={{0,64},{1,65},{2,66},{3,67},{4,68},{5,69},{6,70},{7,71},{8,72},{9,... | collective-permute-start | bytes 1376264 | tf_op jit(solution)/shard_map/ppermute | solution.py:741
  119.4 12.0 %slice-start = ((s8[8388608]{0:T(1024)(128)(4,1)}), s8[4194304]{0:T(1024)(128)(4,1)S(1)}, s32[]{:S(2)}) async-start(s8[8388608]{0:T(1024)(128)(4,1)} %bitcast.130), calls=%async_computation | async-start | bytes 8388608
  119.6 11.9 %slice-start.1 = ((s8[8388608]{0:T(1024)(128)(4,1)}), s8[4194304]{0:T(1024)(128)(4,1)S(1)}, s32[]{:S(2)}) async-start(s8[8388608]{0:T(1024)(128)(4,1)} %bitcast.130), calls=%async_computation.1 | async-start | bytes 8388608
  125.5 20.8 %copy-start = (f32[2,112,4224]{2,1,0:T(8,128)}, f32[2,112,4224]{2,1,0:T(8,128)S(1)}, u32[]{:S(2)}) copy-start(f32[2,112,4224]{2,1,0:T(8,128)S(1)} %fusion.59.p_ref) | copy-start | bytes 11354116
  125.5 4.7 %copy-start.3 = (bf16[2,4,2,128,1024]{4,3,2,1,0:T(8,128)(2,1)S(1)}, bf16[2,4,2,128,1024]{4,3,2,1,0:T(8,128)(2,1)}, u32[]{:S(2)}) copy-start(bf16[2,4,2,128,1024]{4,3,2,1,0:T(8,128)(2,1)} %get-tuple-element.26) | copy-start | bytes 12582916
  137.1 21.0 %slice-start.4 = ((s8[8650752]{0:T(1024)(128)(4,1)}), s8[4194304]{0:T(1024)(128)(4,1)S(1)}, s32[]{:S(2)}) async-start(s8[8650752]{0:T(1024)(128)(4,1)} %bitcast.140), calls=%async_computation.4 | async-start | bytes 8388608
  137.1 21.0 %slice-start.5 = ((s8[8650752]{0:T(1024)(128)(4,1)}), s8[262144]{0:T(1024)(128)(4,1)S(1)}, s32[]{:S(2)}) async-start(s8[8650752]{0:T(1024)(128)(4,1)} %bitcast.140), calls=%async_computation.5 | async-start | bytes 524288
  142.5 15.6 %slice-start.6 = ((s8[8650752]{0:T(1024)(128)(4,1)}), s8[4194304]{0:T(1024)(128)(4,1)S(1)}, s32[]{:S(2)}) async-start(s8[8650752]{0:T(1024)(128)(4,1)} %bitcast.140), calls=%async_computation.6 | async-start | bytes 8388608
  162.1 15.0 %collective-permute-start.1 = (bf16[224,1024]{1,0:T(8,128)(2,1)}, bf16[224,1024]{1,0:T(8,128)(2,1)}, u32[]{:S(2)}, u32[]{:S(2)}) collective-permute-start(bf16[224,1024]{1,0:T(8,128)(2,1)} %fusion.26), channel_id=1, source_target_pairs={{64,0},{65,1},{66,2},{67,3},{68,4},{69,5},{70,6},{71,7},{72,8},{73... | collective-permute-start | bytes 1376264 | tf_op jit(solution)/shard_map/ppermute | solution.py:741
  178.4 5.3 %copy-start.18 = (bf16[2,4,2,128,1024]{4,3,2,1,0:T(8,128)(2,1)S(1)}, bf16[2,4,2,128,1024]{4,3,2,1,0:T(8,128)(2,1)}, u32[]{:S(2)}) copy-start(bf16[2,4,2,128,1024]{4,3,2,1,0:T(8,128)(2,1)} %get-tuple-element.28) | copy-start | bytes 12582916
  183.7 5.2 %slice-start.2 = ((s8[8388608]{0:T(1024)(128)(4,1)}), s8[4194304]{0:T(1024)(128)(4,1)S(1)}, s32[]{:S(2)}) async-start(s8[8388608]{0:T(1024)(128)(4,1)} %bitcast.134), calls=%async_computation.2 | async-start | bytes 8388608
  191.8 5.7 %copy-start.10 = (f32[224,1024]{1,0:T(8,128)}, f32[224,1024]{1,0:T(8,128)S(1)}, u32[]{:S(2)}) copy-start(f32[224,1024]{1,0:T(8,128)S(1)} %get-tuple-element.102) | copy-start | bytes 2752516
  191.8 22.8 %slice-start.7 = ((s8[8650752]{0:T(1024)(128)(4,1)}), s8[4194304]{0:T(1024)(128)(4,1)S(1)}, s32[]{:S(2)}) async-start(s8[8650752]{0:T(1024)(128)(4,1)} %bitcast.143), calls=%async_computation.7 | async-start | bytes 8388608
  197.5 17.1 %slice-start.8 = ((s8[8650752]{0:T(1024)(128)(4,1)}), s8[4194304]{0:T(1024)(128)(4,1)S(1)}, s32[]{:S(2)}) async-start(s8[8650752]{0:T(1024)(128)(4,1)} %bitcast.143), calls=%async_computation.8 | async-start | bytes 8388608
  197.8 3.5 %copy-start.4 = (bf16[2,4,2,128,1024]{4,3,2,1,0:T(8,128)(2,1)S(1)}, bf16[2,4,2,128,1024]{4,3,2,1,0:T(8,128)(2,1)}, u32[]{:S(2)}) copy-start(bf16[2,4,2,128,1024]{4,3,2,1,0:T(8,128)(2,1)} %get-tuple-element.26) | copy-start | bytes 12582916
  201.3 13.3 %slice-start.9 = ((s8[8650752]{0:T(1024)(128)(4,1)}), s8[262144]{0:T(1024)(128)(4,1)S(1)}, s32[]{:S(2)}) async-start(s8[8650752]{0:T(1024)(128)(4,1)} %bitcast.143), calls=%async_computation.9 | async-start | bytes 524288
  314.6 6.9 %copy-start.11 = (f32[224,1024]{1,0:T(8,128)S(1)}, f32[224,1024]{1,0:T(8,128)}, u32[]{:S(2)}) copy-start(f32[224,1024]{1,0:T(8,128)} %copy-done.10) | copy-start | bytes 2752516
  314.6 6.9 %copy-start.12 = (f32[224,1024]{1,0:T(8,128)S(1)}, f32[224,1024]{1,0:T(8,128)}, u32[]{:S(2)}) copy-start(f32[224,1024]{1,0:T(8,128)} %get-tuple-element.103) | copy-start | bytes 2752516
  317.3 5.7 %copy-start.13 = (bf16[128,1024]{1,0:T(8,128)(2,1)S(1)}, bf16[128,1024]{1,0:T(8,128)(2,1)}, u32[]{:S(2)}) copy-start(bf16[128,1024]{1,0:T(8,128)(2,1)} %get-tuple-element.38) | copy-start | bytes 786436
  317.3 5.7 %copy-start.14 = (bf16[128,1024]{1,0:T(8,128)(2,1)S(1)}, bf16[128,1024]{1,0:T(8,128)(2,1)}, u32[]{:S(2)}) copy-start(bf16[128,1024]{1,0:T(8,128)(2,1)} %get-tuple-element.40) | copy-start | bytes 786436
  319.4 4.7 %copy-start.15 = (f32[2,64]{1,0:T(2,128)S(1)}, f32[2,64]{1,0:T(2,128)}, u32[]{:S(2)}) copy-start(f32[2,64]{1,0:T(2,128)} %get-tuple-element.34) | copy-start | bytes 1540
  (7 other events, 17.3 us)

commit v2 on v1

--- a/solution.py
+++ b/solution.py
@@ -472,7 +472,7 @@
         loads.append(load)
 
     plans = [schedule(order, y, z, x) for _, _, _, order in SCATTERED]
-    flying = {}
+    flying, last = {}, []
     sems = 0
     for stage in range(len(HOPS) + 1):
         for p, (array, column, columns, order) in enumerate(SCATTERED):
@@ -505,23 +505,23 @@
                     copies.append(copy)
                     sems += 1
                 flying[p, stage] = copies
-
-    last = []
-    for array in range(4):
-        quarter = SHARD_ROWS[array] // 4
-        mine = pl.ds(pl.multiple_of(x * quarter, quarter), quarter)
-        for k, name in enumerate(("xo", "xa", "xb")):
-            copy = pltpu.make_async_remote_copy(
-                src_ref=accs[array].at[y, z, mine],
-                dst_ref=wholes[array].at[mine],
-                send_sem=last_send.at[array, k],
-                recv_sem=last_recv.at[array, k],
-                device_id=near[name],
-                device_id_type=MESH,
-            )
-            copy.start()
-            last.append(copy)
-        wholes[array][mine, :] = accs[array][y, z, mine, :]
+                continue
+            if p + 1 < len(SCATTERED) and SCATTERED[p + 1][0] == array:
+                continue
+            mine = pl.ds(pl.multiple_of(x * quarter, quarter), quarter)
+            for k, name in enumerate(("xo", "xa", "xb")):
+                copy = pltpu.make_async_remote_copy(
+                    src_ref=accs[array].at[y, z, mine],
+                    dst_ref=wholes[array].at[mine],
+                    send_sem=last_send.at[array, k],
+                    recv_sem=last_recv.at[array, k],
+                    device_id=near[name],
+                    device_id_type=MESH,
+                )
+                copy.start()
+                last.append(copy)
+            wholes[array][mine, :] = accs[array][y, z, mine, :]
+
     for copy in last:
         copy.wait_recv()
     small = wholes[0][:, EXTRA:].astype(F32)

time: 330 us -> 327 us (level)
  no operation moved by 1% of the time
where the time goes in v2:
time: 327 us; the launch traced here: 322 us
  Pallas kernels  196 us (60%)
  matrix products  70.7 us (22%)
  waiting for transfers between devices  23.3 us (7%)
  other arithmetic  15.1 us (5%)
  local copies, waits for them, and re-layouts  8.76 us (3%)
  starting transfers between devices  6.3 us (2%)
    pallas_call x1, Pallas kernels, scatter_sums(): pl.pallas_call(scatter_kernel, in_specs=[pl.BlockSpec(memory_space=pl.ANY...  86 us
    pallas_call x1, Pallas kernels, gather_shards(): pl.pallas_call(gather_kernel, in_specs=[pl.BlockSpec(memory_space=pl.ANY)...  78 us
    dot_general x8, matrix products, back_product(): lax.dot_general(grad_rows, weight, (((1,), (1,)), ((), ())), preferred_el...  27.5 us
    dot_general x8, matrix products, forward_product(): return jnp.dot(left, weight, preferred_element_type=F32)  25 us
    ppermute x2, waiting for transfers between devices, across(): return lax.ppermute(array, 'section', [(0, 1)] if by > 0 else [(1, 0)])  23.3 us
    pallas_call x2, Pallas kernels, mix_backward(): pl.pallas_call(mix_backward_kernel, grid=(blocks,), in_specs=[per_block((...  22.8 us
    dot_general x4, matrix products, outer_sum(): lax.dot_general(left, right, (((0,), (0,)), ((), ())), preferred_element_...  18.2 us
    pallas_call x2, Pallas kernels, mix_forward(): pl.pallas_call(mix_forward_kernel, grid=(blocks,), in_specs=[per_block((T...  9.33 us
  transfers between devices with their start and end apart: 2, of which 2 were waited for; matrix products, arithmetic and copies ran while one was open for 0% of the time, Pallas kernels for 0%

profile of v2, /device:TPU:1, one launch (start us, length us, event | category | flops | bytes accessed | tf_op | source)
XLA Modules:
  0.0 321.8 jit_solution(13962306316038951357)
XLA Ops:
  3.6 78.0 %gather_shards.1 = (bf16[2,4,2,64,4224]{4,3,2,1,0:T(8,128)(2,1)}, bf16[2,4,2,128,1024]{4,3,2,1,0:T(8,128)(2,1)}, bf16[2,4,2,64,4096]{4,3,2,1,0:T(8,128)(2,1)}, bf16[2,4,2,128,1024]{4,3,2,1,0:T(8,128)(2,1)}) custom-call(bf16[1,1,1,64,4120]{4,3,2,1,0:T(8,128)(2,1)} %bitcast.161, bf16[1,1,1,128,1024]{4,3,2,1,0:T(8,128)(2,1)} %bitcast.164, ...), custom_call_target="tpu_custom_call" | custom-call | tf_op jit(solution)/shard_map/gather_shards/pallas_call | solution.py:649
  85.9 5.7 %fusion.35.p_ref = f32[2,112,4224]{2,1,0:T(8,128)S(1)} fusion(bf16[1024,4224,1]{1,0,2:T(8,128)(2,1)} %bitcast.138, bf16[2,112,1024]{2,1,0:T(8,128)(2,1)S(1)} %copy-done.6, f32[1024]{0:T(1024)S(1)} %mul.119, f32[2,112]{1,0:T(2,128)S(1)} %add_rsqrt_fusion.3), kind=kOutput, calls=%fused_computation.66 | convolution fusion | flops 1938685952 | bytes 12899200 | tf_op jit(solution)/shard_map/dot_general | solution.py:681
  91.8 4.6 %mix_forward.2 = bf16[2,112,2048]{2,1,0:T(8,128)(2,1)S(1)} custom-call(f32[2,112,4224]{2,1,0:T(8,128)S(1)} %fusion.35.p_ref, f32[2,112,128]{2,1,0:T(8,128)S(1)} %broadcast_in_dim.18.segc_ref, f32[2,8,112]{2,1,0:T(8,128)S(1)} %broadcast_in_dim.19.segr_ref, f32[8,1792]{1,0:T(8,128)S(1)} %pad.38.conv_ref, f32[8,128]{1,0:T(8,128)S(1)} %pad.39.head_ref, ...), custom_call_target="tpu_custom_call" | custom-call | tf_op jit(solution)/shard_map/mix_forward/pallas_call | solution.py:261
  97.6 5.7 %fusion.34 = f32[224,4096]{1,0:T(8,128)S(1)} fusion(bf16[1024,4096]{1,0:T(8,128)(2,1)} %bitcast.129, f32[224,1024]{1,0:T(8,128)S(1)} %get-tuple-element.95, f32[1024]{0:T(1024)S(1)} %mul.125, f32[224]{0:T(256)S(1)} %add_rsqrt_fusion.2), kind=kOutput, calls=%fused_computation.65 | convolution fusion | flops 1879736320 | bytes 12981120 | tf_op jit(solution)/shard_map/dot_general | solution.py:681
  104.6 4.8 %collective-permute-start = (bf16[224,1024]{1,0:T(8,128)(2,1)S(1)}, bf16[224,1024]{1,0:T(8,128)(2,1)S(1)}, u32[]{:S(2)}, u32[]{:S(2)}) collective-permute-start(bf16[224,1024]{1,0:T(8,128)(2,1)S(1)} %fusion.15), channel_id=1, source_target_pairs={{0,64},{1,65},{2,66},{3,67},{4,68},{5,69},{6,70},{7,71},{8,72},{9,... | collective-permute-start | bytes 1376264 | tf_op jit(solution)/shard_map/ppermute | solution.py:741
  109.5 9.7 %collective-permute-done = bf16[224,1024]{1,0:T(8,128)(2,1)S(1)} collective-permute-done((bf16[224,1024]{1,0:T(8,128)(2,1)S(1)}, bf16[224,1024]{1,0:T(8,128)(2,1)S(1)}, u32[]{:S(2)}, u32[]{:S(2)}) %collective-permute-start) | collective-permute-done | bytes 458784 | tf_op jit(solution)/shard_map/ppermute | solution.py:741
  119.6 5.8 %fusion.59.p_ref = f32[2,112,4224]{2,1,0:T(8,128)S(1)} fusion(bf16[2,112,1024]{2,1,0:T(8,128)(2,1)S(1)} %bitcast.153, bf16[1024,4224,1]{1,0,2:T(8,128)(2,1)} %bitcast.139), kind=kOutput, calls=%fused_computation.120 | convolution fusion | flops 1937768448 | bytes 12894208 | tf_op jit(solution)/shard_map/dot_general | solution.py:681
  125.5 4.7 %mix_forward.3 = bf16[2,112,2048]{2,1,0:T(8,128)(2,1)S(1)} custom-call(f32[2,112,4224]{2,1,0:T(8,128)S(1)} %fusion.59.p_ref, f32[2,112,128]{2,1,0:T(8,128)S(1)} %broadcast_in_dim.18.segc_ref, f32[2,8,112]{2,1,0:T(8,128)S(1)} %broadcast_in_dim.19.segr_ref, f32[8,1792]{1,0:T(8,128)S(1)} %pad.38.conv_ref, f32[8,128]{1,0:T(8,128)S(1)} %pad.39.head_ref, ...), custom_call_target="tpu_custom_call" | custom-call | tf_op jit(solution)/shard_map/mix_forward/pallas_call | solution.py:261
  131.5 2.2 fusion.55
  133.8 3.2 %multiply_convert_fusion.3 = (bf16[224,2048]{1,0:T(8,128)(2,1)}, bf16[224,2048]{1,0:T(8,128)(2,1)}) fusion(f32[224,4096]{1,0:T(8,128)S(1)} %fusion.55, bf16[2048,1024]{1,0:T(8,128)(2,1)S(1)} %bitcast.180, bf16[224,1024]{1,0:T(8,128)(2,1)S(1)} %bitcast.154), kind=kOutput, calls=%fused_computation.15 | convolution fusion | flops 945487872 | bytes 10158080 | tf_op jit(solution)/shard_map/dot_general | solution.py:685
  137.1 4.4 %multiply_reduce_fusion.2 = (f32[224]{0:T(256)S(1)}, f32[224,1024]{1,0:T(8,128)S(1)}) fusion(f32[224,1024]{1,0:T(8,128)S(1)} %get-tuple-element.97, f32[224]{0:T(256)S(1)} %add_rsqrt_fusion, f32[1024]{0:T(1024)S(1)} %mul.125, bf16[1024,4096]{1,0:T(8,128)(2,1)S(1)} %bitcast.133, bf16[224,2048]{1,0:T(8,128)(2,1)} %get-tuple-element.88, ...), kind=kOutput, calls=%fused_computation.58 | convolution fusion | flops 1883635456 | bytes 12064512 | tf_op jit(solution)/shard_map/dot_general | solution.py:685
  142.5 3.7 %fusion.60.gu_ref = f32[2,112,2048]{2,1,0:T(8,128)S(1)} fusion(bf16[2,112,1024]{2,1,0:T(8,128)(2,1)S(1)} %bitcast.158, bf16[2048,1024,1]{1,0,2:T(8,128)(2,1)} %bitcast.149), kind=kOutput, calls=%fused_computation.121 | convolution fusion | flops 939524096 | bytes 6488064 | tf_op jit(solution)/shard_map/dot_general | solution.py:685
  146.2 11.8 %mix_backward.2 = (bf16[2,112,4224]{2,1,0:T(8,128)(2,1)S(1)}, f32[2,8,1792]{2,1,0:T(8,128)}, f32[2,8,128]{2,1,0:T(8,128)}, f32[2,8,1536]{2,1,0:T(8,128)}) custom-call(f32[2,112,4224]{2,1,0:T(8,128)S(1)} %fusion.59.p_ref, f32[2,112,2048]{2,1,0:T(8,128)S(1)} %fusion.60.gu_ref, f32[2,112,128]{2,1,0:T(8,128)S(1)} %broadcast_in_dim.18.segc_ref, ...), custom_call_target="tpu_custom_call" | custom-call | tf_op jit(solution)/shard_map/mix_backward/pallas_call | solution.py:275
  158.1 2.8 fusion.22
  163.6 13.6 %collective-permute-done.1 = bf16[224,1024]{1,0:T(8,128)(2,1)} collective-permute-done((bf16[224,1024]{1,0:T(8,128)(2,1)}, bf16[224,1024]{1,0:T(8,128)(2,1)}, u32[]{:S(2)}, u32[]{:S(2)}) %collective-permute-start.1) | collective-permute-done | bytes 458784 | tf_op jit(solution)/shard_map/ppermute | solution.py:741
  178.4 5.3 %multiply_convert_fusion.1 = (bf16[224,2048]{1,0:T(8,128)(2,1)S(1)}, bf16[224,2048]{1,0:T(8,128)(2,1)S(1)}, bf16[224,2048]{1,0:T(8,128)(2,1)S(1)}) fusion(f32[224,4096]{1,0:T(8,128)} %copy-done.7, bf16[224,1024]{1,0:T(8,128)(2,1)S(1)} %broadcast_select_fusion, bf16[2048,1024]{1,0:T(8,128)(2,1)} %bitcast.178), kind=kOutput, calls=%fused_computation.13 | convolution fusion | flops 946405376 | bytes 11075584 | tf_op jit(solution)/shard_map/dot_general | solution.py:685
  185.7 3.2 %convolution_convert_fusion.2 = bf16[2048,1024]{1,0:T(8,128)(2,1)} fusion(bf16[224,2048]{1,0:T(8,128)(2,1)S(1)} %get-tuple-element.89, bf16[224,1024]{1,0:T(8,128)(2,1)S(1)} %broadcast_select_fusion), kind=kOutput, calls=%fused_computation.2 | convolution fusion | flops 941621248 | bytes 5570560 | tf_op jit(solution)/shard_map/dot_general | solution.py:691
  188.9 2.9 multiply_reduce_fusion
  191.8 5.7 %convolution_convert_fusion.1 = bf16[1024,4096]{1,0:T(8,128)(2,1)} fusion(bf16[224,2048]{1,0:T(8,128)(2,1)S(1)} %get-tuple-element.86, bf16[224,2048]{1,0:T(8,128)(2,1)S(1)} %get-tuple-element.85, f32[224,1024]{1,0:T(8,128)S(1)} %get-tuple-element.97, f32[224]{0:T(256)S(1)} %add_rsqrt_fusion, f32[1024]{0:T(1024)S(1)} %mul.125), kind=kOutput, calls=%fused_computation.1 | convolution fusion | flops 1887600640 | bytes 11146112 | tf_op jit(solution)/shard_map/dot_general | solution.py:691
  197.8 3.5 %convolution_convert_fusion.3 = bf16[2048,1024]{1,0:T(8,128)(2,1)} fusion(bf16[224,2048]{1,0:T(8,128)(2,1)S(1)} %bitcast.124, bf16[224,1024]{1,0:T(8,128)(2,1)S(1)} %fusion.57), kind=kOutput, calls=%fused_computation.3 | convolution fusion | flops 941621248 | bytes 5570560 | tf_op jit(solution)/shard_map/dot_general | solution.py:691
  203.6 10.9 %mix_backward.3 = (bf16[2,112,4224]{2,1,0:T(8,128)(2,1)S(1)}, f32[2,8,1792]{2,1,0:T(8,128)S(1)}, f32[2,8,128]{2,1,0:T(8,128)S(1)}, f32[2,8,1536]{2,1,0:T(8,128)S(1)}) custom-call(f32[2,112,4224]{2,1,0:T(8,128)S(1)} %copy-done.1, f32[2,112,2048]{2,1,0:T(8,128)S(1)} %fusion.61.gu_ref, f32[2,112,128]{2,1,0:T(8,128)S(1)} %broadcast_in_dim.18.segc_ref, ...), custom_call_target="tpu_custom_call" | custom-call | tf_op jit(solution)/shard_map/mix_backward/pallas_call | solution.py:275
  214.6 3.6 %fusion.31 = (bf16[1024]{0:T(1024)(128)(2,1)S(1)}, f32[224]{0:T(256)S(1)}, f32[224,1024]{1,0:T(8,128)}) fusion(bf16[224,1024]{1,0:T(8,128)(2,1)S(1)} %get-tuple-element.84, f32[224]{0:T(256)S(1)} %add_rsqrt_fusion.1, f32[1024]{0:T(1024)S(1)} %mul.119, bf16[224,4224]{1,0:T(8,128)(2,1)S(1)} %bitcast.125, bf16[1024,4224]{1,0:T(8,128)(2,1)S(1)} %bitcast.145), kind=kOutput, calls=%fused_computation.52 | convolution fusion | flops 1939372800 | bytes 11927296 | tf_op jit(solution)/shard_map/dot_general | solution.py:685
  218.2 5.9 %convolution_convert_fusion = bf16[1024,4224]{1,0:T(8,128)(2,1)} fusion(bf16[224,1024]{1,0:T(8,128)(2,1)S(1)} %fusion.21, bf16[224,4224]{1,0:T(8,128)(2,1)S(1)} %bitcast.126), kind=kOutput, calls=%fused_computation | convolution fusion | flops 1942093824 | bytes 11001856 | tf_op jit(solution)/shard_map/dot_general | solution.py:691
  225.6 86.0 %scatter_sums.1 = (bf16[64,4352]{1,0:T(8,128)(2,1)}, bf16[128,1024]{1,0:T(8,128)(2,1)}, bf16[64,4096]{1,0:T(8,128)(2,1)}, bf16[128,1024]{1,0:T(8,128)(2,1)}, f32...) custom-call(bf16[2,4,2,64,4224]{4,3,2,1,0:T(8,128)(2,1)} %bitcast.137, bf16[2,4,2,128,1024]{4,3,2,1,0:T(8,128)(2,1)} %bitcast.148, ...), custom_call_target="tpu_custom_call" | custom-call | tf_op jit(solution)/shard_map/scatter_sums/pallas_call | solution.py:544
  (132 shorter events, 32.4 us)
Async XLA Ops:
  0.6 85.3 %copy-start.6 = (bf16[2,112,1024]{2,1,0:T(8,128)(2,1)S(1)}, bf16[2,112,1024]{2,1,0:T(8,128)(2,1)}, u32[]{:S(2)}) copy-start(bf16[2,112,1024]{2,1,0:T(8,128)(2,1)} %param.10) | copy-start | bytes 1376260
  91.6 4.8 %copy-start.2 = (bf16[2,4,2,128,1024]{4,3,2,1,0:T(8,128)(2,1)S(1)}, bf16[2,4,2,128,1024]{4,3,2,1,0:T(8,128)(2,1)}, u32[]{:S(2)}) copy-start(bf16[2,4,2,128,1024]{4,3,2,1,0:T(8,128)(2,1)} %get-tuple-element.26) | copy-start | bytes 12582916
  97.6 5.7 %copy-start.16 = (bf16[2,4,2,128,1024]{4,3,2,1,0:T(8,128)(2,1)S(1)}, bf16[2,4,2,128,1024]{4,3,2,1,0:T(8,128)(2,1)}, u32[]{:S(2)}) copy-start(bf16[2,4,2,128,1024]{4,3,2,1,0:T(8,128)(2,1)} %get-tuple-element.28) | copy-start | bytes 12582916
  104.6 14.6 %collective-permute-start = (bf16[224,1024]{1,0:T(8,128)(2,1)S(1)}, bf16[224,1024]{1,0:T(8,128)(2,1)S(1)}, u32[]{:S(2)}, u32[]{:S(2)}) collective-permute-start(bf16[224,1024]{1,0:T(8,128)(2,1)S(1)} %fusion.15), channel_id=1, source_target_pairs={{0,64},{1,65},{2,66},{3,67},{4,68},{5,69},{6,70},{7,71},{8,72},{9,... | collective-permute-start | bytes 1376264 | tf_op jit(solution)/shard_map/ppermute | solution.py:741
  119.4 12.0 %slice-start = ((s8[8388608]{0:T(1024)(128)(4,1)}), s8[4194304]{0:T(1024)(128)(4,1)S(1)}, s32[]{:S(2)}) async-start(s8[8388608]{0:T(1024)(128)(4,1)} %bitcast.130), calls=%async_computation | async-start | bytes 8388608
  119.6 11.9 %slice-start.1 = ((s8[8388608]{0:T(1024)(128)(4,1)}), s8[4194304]{0:T(1024)(128)(4,1)S(1)}, s32[]{:S(2)}) async-start(s8[8388608]{0:T(1024)(128)(4,1)} %bitcast.130), calls=%async_computation.1 | async-start | bytes 8388608
  125.5 20.8 %copy-start = (f32[2,112,4224]{2,1,0:T(8,128)}, f32[2,112,4224]{2,1,0:T(8,128)S(1)}, u32[]{:S(2)}) copy-start(f32[2,112,4224]{2,1,0:T(8,128)S(1)} %fusion.59.p_ref) | copy-start | bytes 11354116
  125.5 4.7 %copy-start.3 = (bf16[2,4,2,128,1024]{4,3,2,1,0:T(8,128)(2,1)S(1)}, bf16[2,4,2,128,1024]{4,3,2,1,0:T(8,128)(2,1)}, u32[]{:S(2)}) copy-start(bf16[2,4,2,128,1024]{4,3,2,1,0:T(8,128)(2,1)} %get-tuple-element.26) | copy-start | bytes 12582916
  137.1 21.0 %slice-start.4 = ((s8[8650752]{0:T(1024)(128)(4,1)}), s8[4194304]{0:T(1024)(128)(4,1)S(1)}, s32[]{:S(2)}) async-start(s8[8650752]{0:T(1024)(128)(4,1)} %bitcast.140), calls=%async_computation.4 | async-start | bytes 8388608
  137.1 21.0 %slice-start.5 = ((s8[8650752]{0:T(1024)(128)(4,1)}), s8[262144]{0:T(1024)(128)(4,1)S(1)}, s32[]{:S(2)}) async-start(s8[8650752]{0:T(1024)(128)(4,1)} %bitcast.140), calls=%async_computation.5 | async-start | bytes 524288
  142.5 15.6 %slice-start.6 = ((s8[8650752]{0:T(1024)(128)(4,1)}), s8[4194304]{0:T(1024)(128)(4,1)S(1)}, s32[]{:S(2)}) async-start(s8[8650752]{0:T(1024)(128)(4,1)} %bitcast.140), calls=%async_computation.6 | async-start | bytes 8388608
  162.1 15.0 %collective-permute-start.1 = (bf16[224,1024]{1,0:T(8,128)(2,1)}, bf16[224,1024]{1,0:T(8,128)(2,1)}, u32[]{:S(2)}, u32[]{:S(2)}) collective-permute-start(bf16[224,1024]{1,0:T(8,128)(2,1)} %fusion.26), channel_id=1, source_target_pairs={{64,0},{65,1},{66,2},{67,3},{68,4},{69,5},{70,6},{71,7},{72,8},{73... | collective-permute-start | bytes 1376264 | tf_op jit(solution)/shard_map/ppermute | solution.py:741
  178.4 5.3 %copy-start.18 = (bf16[2,4,2,128,1024]{4,3,2,1,0:T(8,128)(2,1)S(1)}, bf16[2,4,2,128,1024]{4,3,2,1,0:T(8,128)(2,1)}, u32[]{:S(2)}) copy-start(bf16[2,4,2,128,1024]{4,3,2,1,0:T(8,128)(2,1)} %get-tuple-element.28) | copy-start | bytes 12582916
  183.7 5.2 %slice-start.2 = ((s8[8388608]{0:T(1024)(128)(4,1)}), s8[4194304]{0:T(1024)(128)(4,1)S(1)}, s32[]{:S(2)}) async-start(s8[8388608]{0:T(1024)(128)(4,1)} %bitcast.134), calls=%async_computation.2 | async-start | bytes 8388608
  191.8 5.7 %copy-start.10 = (f32[224,1024]{1,0:T(8,128)}, f32[224,1024]{1,0:T(8,128)S(1)}, u32[]{:S(2)}) copy-start(f32[224,1024]{1,0:T(8,128)S(1)} %get-tuple-element.102) | copy-start | bytes 2752516
  191.8 22.8 %slice-start.7 = ((s8[8650752]{0:T(1024)(128)(4,1)}), s8[4194304]{0:T(1024)(128)(4,1)S(1)}, s32[]{:S(2)}) async-start(s8[8650752]{0:T(1024)(128)(4,1)} %bitcast.143), calls=%async_computation.7 | async-start | bytes 8388608
  197.5 17.1 %slice-start.8 = ((s8[8650752]{0:T(1024)(128)(4,1)}), s8[4194304]{0:T(1024)(128)(4,1)S(1)}, s32[]{:S(2)}) async-start(s8[8650752]{0:T(1024)(128)(4,1)} %bitcast.143), calls=%async_computation.8 | async-start | bytes 8388608
  197.8 3.5 %copy-start.4 = (bf16[2,4,2,128,1024]{4,3,2,1,0:T(8,128)(2,1)S(1)}, bf16[2,4,2,128,1024]{4,3,2,1,0:T(8,128)(2,1)}, u32[]{:S(2)}) copy-start(bf16[2,4,2,128,1024]{4,3,2,1,0:T(8,128)(2,1)} %get-tuple-element.26) | copy-start | bytes 12582916
  201.3 13.3 %slice-start.9 = ((s8[8650752]{0:T(1024)(128)(4,1)}), s8[262144]{0:T(1024)(128)(4,1)S(1)}, s32[]{:S(2)}) async-start(s8[8650752]{0:T(1024)(128)(4,1)} %bitcast.143), calls=%async_computation.9 | async-start | bytes 524288
  311.6 6.9 %copy-start.11 = (f32[224,1024]{1,0:T(8,128)S(1)}, f32[224,1024]{1,0:T(8,128)}, u32[]{:S(2)}) copy-start(f32[224,1024]{1,0:T(8,128)} %copy-done.10) | copy-start | bytes 2752516
  311.6 6.9 %copy-start.12 = (f32[224,1024]{1,0:T(8,128)S(1)}, f32[224,1024]{1,0:T(8,128)}, u32[]{:S(2)}) copy-start(f32[224,1024]{1,0:T(8,128)} %get-tuple-element.103) | copy-start | bytes 2752516
  314.2 5.7 %copy-start.13 = (bf16[128,1024]{1,0:T(8,128)(2,1)S(1)}, bf16[128,1024]{1,0:T(8,128)(2,1)}, u32[]{:S(2)}) copy-start(bf16[128,1024]{1,0:T(8,128)(2,1)} %get-tuple-element.38) | copy-start | bytes 786436
  314.2 5.7 %copy-start.14 = (bf16[128,1024]{1,0:T(8,128)(2,1)S(1)}, bf16[128,1024]{1,0:T(8,128)(2,1)}, u32[]{:S(2)}) copy-start(bf16[128,1024]{1,0:T(8,128)(2,1)} %get-tuple-element.40) | copy-start | bytes 786436
  316.4 4.7 %copy-start.15 = (f32[2,64]{1,0:T(2,128)S(1)}, f32[2,64]{1,0:T(2,128)}, u32[]{:S(2)}) copy-start(f32[2,64]{1,0:T(2,128)} %get-tuple-element.34) | copy-start | bytes 1540
  (7 other events, 17.3 us)

commit v3 on v2

--- a/solution.py
+++ b/solution.py
@@ -110,7 +110,8 @@
     return jnp.where(left, tile, turned), jnp.where(left, turned, tile)
 
 
-def mix_forward_kernel(p_ref, segc_ref, segr_ref, conv_ref, head_ref, skip_ref, u_ref, act_ref):
+def mix_forward_kernel(p_ref, segc_ref, segr_ref, conv_ref, head_ref, skip_ref, u_ref, *rest):
+    y_ref, act_ref = rest if len(rest) == 2 else (None, *rest)
     allowed, links = block_masks(segc_ref[0], segr_ref[0])
     convolve(p_ref, conv_ref, links, None, act_ref)
     _, dt, _, cum = steps_and_sums(p_ref, head_ref)
@@ -125,6 +126,8 @@
             decayed = jnp.exp(jnp.where(allowed, cum[:, h : h + 1] - cum_t[h : h + 1, :], -1e30))
             parts.append((decayed * cb * dt_t[h : h + 1, :]).astype(BF16))
         y = picked(dot_nn(jnp.concatenate(parts, 0), xs), left) + skip_ref[0:1, sl] * xs
+        if y_ref is not None:
+            y_ref[0, :, sl] = y
         z = p_ref[0, :, sl]
         u_ref[0, :, sl] = (y * (z * jax.nn.sigmoid(z))).astype(BF16)
     k_dups = [tile.astype(BF16) for tile in doubled(p_ref[0, :, OFF_K:OFF_V], left)]
@@ -144,7 +147,7 @@
 
 
 def mix_backward_kernel(
-    p_ref, gu_ref, segc_ref, segr_ref, conv_ref, head_ref, skip_ref,
+    p_ref, gu_ref, y_ref, segc_ref, segr_ref, conv_ref, head_ref, skip_ref,
     gp_ref, gconv_ref, ghead_ref, gskip_ref,
     mixed_ref, act_ref, gact_ref, colq_ref,
 ):
@@ -183,7 +186,7 @@
             row_form = jnp.where(lanes == h, jnp.sum(q * dt_row, 1, keepdims=True), row_form)
         skip = skip_ref[0:1, sl]
         kernels = jnp.concatenate(parts, 0)
-        y = picked(dot_nn(kernels, xs16), left) + skip * xs
+        y = y_ref[0, :, sl]
         gp_ref[0, :, sl] = (gm * y * (sg * (1.0 + z * (1.0 - sg)))).astype(BF16)
         gact_ref[:, sl] = dot_tn(kernels, gy_stack) + skip * gy
         gskip_ref[0, 0:1, sl] = jnp.sum(gy * xs, 0, keepdims=True)
@@ -256,26 +259,27 @@
     ]
 
 
-def mix_forward(projected, tables):
+def mix_forward(projected, tables, keep):
     blocks = projected.shape[0]
+    widths = ((UW, BF16), (SSM, F32))[: 1 + keep]
     return pl.pallas_call(
         mix_forward_kernel,
         grid=(blocks,),
         in_specs=[per_block((T, PAD)), *small_specs()],
-        out_specs=per_block((T, UW)),
-        out_shape=jax.ShapeDtypeStruct((blocks, T, UW), BF16),
+        out_specs=[per_block((T, width)) for width, _ in widths],
+        out_shape=[jax.ShapeDtypeStruct((blocks, T, width), kind) for width, kind in widths],
         scratch_shapes=[pltpu.VMEM((T, CH), F32)],
         compiler_params=pltpu.CompilerParams(vmem_limit_bytes=32 * 1024 * 1024),
         name="mix_forward",
     )(projected, *tables)
 
 
-def mix_backward(projected, grad_joined, tables):
+def mix_backward(projected, grad_joined, kept, tables):
     blocks = projected.shape[0]
     return pl.pallas_call(
         mix_backward_kernel,
         grid=(blocks,),
-        in_specs=[per_block((T, PAD)), per_block((T, UW)), *small_specs()],
+        in_specs=[per_block((T, PAD)), per_block((T, UW)), per_block((T, SSM)), *small_specs()],
         out_specs=[per_block((T, PAD)), per_block((8, CH)), per_block((8, 128)), per_block((8, SSM))],
         out_shape=[
             jax.ShapeDtypeStruct((blocks, T, PAD), BF16),
@@ -291,7 +295,7 @@
         ],
         compiler_params=pltpu.CompilerParams(vmem_limit_bytes=40 * 1024 * 1024),
         name="mix_backward",
-    )(projected, grad_joined, *tables)
+    )(projected, grad_joined, kept, *tables)
 
 
 def mixer_tables(segments, conv_rows, head_table):
@@ -693,23 +697,24 @@
     ).astype(BF16)
 
 
-def layer_forward(inputs, weights, tables):
+def layer_forward(inputs, weights, tables, keep):
     gains, w_in, w_out, w_gate_up, w_down = weights
     blocks = inputs.shape[0] // T
     normed = rms_norm(inputs, gains[0]).astype(BF16)
     projected = forward_product(normed, w_in)
-    joined = mix_forward(projected.reshape(blocks, T, PAD), tables).reshape(blocks * T, UW)
+    joined, *kept = mix_forward(projected.reshape(blocks, T, PAD), tables, keep)
+    joined = joined.reshape(blocks * T, UW)
     hidden = inputs + forward_product(joined, w_out)
     normed_two = rms_norm(hidden, gains[1]).astype(BF16)
     gate_up = forward_product(normed_two, w_gate_up)
     activated = (jax.nn.silu(gate_up[:, :FF]) * gate_up[:, FF:]).astype(BF16)
     result = hidden + forward_product(activated, w_down)
-    return result, (inputs, normed, projected, joined, hidden, normed_two, gate_up, activated)
+    return result, (inputs, normed, projected, joined, hidden, normed_two, gate_up, activated, *kept)
 
 
 def layer_backward(grad_out, saved, weights, tables):
     gains, w_in, w_out, w_gate_up, w_down = weights
-    inputs, normed, projected, joined, hidden, normed_two, gate_up, activated = saved
+    inputs, normed, projected, joined, hidden, normed_two, gate_up, activated, kept = saved
     blocks = inputs.shape[0] // T
     grad_ffn = grad_out.astype(BF16)
     grad_act = back_product(grad_ffn, w_down)
@@ -723,7 +728,7 @@
     grad_branch = grad_hidden.astype(BF16)
     grad_joined = back_product(grad_branch, w_out)
     grad_proj, grad_conv, grad_head, grad_skip = mix_backward(
-        projected.reshape(blocks, T, PAD), grad_joined.reshape(blocks, T, UW), tables
+        projected.reshape(blocks, T, PAD), grad_joined.reshape(blocks, T, UW), kept, tables
     )
     grad_proj = grad_proj.reshape(blocks * T, PAD)
     grad_input, grad_gain_one = rms_back(inputs, gains[0], back_product(grad_proj, w_in))
@@ -786,10 +791,10 @@
     tables = mixer_tables(segment_ids[:, 0], conv_rows, head_params[0].astype(F32))
 
     own = tokens.reshape(rows, width)
-    first, _ = layer_forward(own.astype(F32), weights, tables)
+    first, _ = layer_forward(own.astype(F32), weights, tables, False)
     received = across(first.astype(BF16), 1)
     inputs = jnp.where(section == 0, own, received).astype(F32)
-    result, saved = layer_forward(inputs, weights, tables)
+    result, saved = layer_forward(inputs, weights, tables, True)
 
     top = cotangent.reshape(rows, width)
     first_grad, _, _ = layer_backward(top.astype(F32), saved, weights, tables)

time: 327 us -> 325 us (level)
  no operation moved by 1% of the time
where the time goes in v3:
time: 325 us; the launch traced here: 319 us
  Pallas kernels  196 us (60%)
  matrix products  68.4 us (21%)
  waiting for transfers between devices  23.3 us (7%)
  other arithmetic  15.1 us (5%)
  local copies, waits for them, and re-layouts  8.18 us (3%)
  starting transfers between devices  6.3 us (2%)
    pallas_call x1, Pallas kernels, scatter_sums(): pl.pallas_call(scatter_kernel, in_specs=[pl.BlockSpec(memory_space=pl.ANY...  86 us
    pallas_call x1, Pallas kernels, gather_shards(): pl.pallas_call(gather_kernel, in_specs=[pl.BlockSpec(memory_space=pl.ANY)...  78 us
    dot_general x8, matrix products, forward_product(): return jnp.dot(left, weight, preferred_element_type=F32)  25.5 us
    dot_general x8, matrix products, back_product(): lax.dot_general(grad_rows, weight, (((1,), (1,)), ((), ())), preferred_el...  24.6 us
    ppermute x2, waiting for transfers between devices, across(): return lax.ppermute(array, 'section', [(0, 1)] if by > 0 else [(1, 0)])  23.3 us
    pallas_call x2, Pallas kernels, mix_backward(): pl.pallas_call(mix_backward_kernel, grid=(blocks,), in_specs=[per_block((...  22.8 us
    dot_general x4, matrix products, outer_sum(): lax.dot_general(left, right, (((0,), (0,)), ((), ())), preferred_element_...  18.3 us
    pallas_call x2, Pallas kernels, mix_forward(): pl.pallas_call(mix_forward_kernel, grid=(blocks,), in_specs=[per_block((T...  9.35 us
  transfers between devices with their start and end apart: 2, of which 2 were waited for; matrix products, arithmetic and copies ran while one was open for 0% of the time, Pallas kernels for 0%

profile of v3, /device:TPU:1, one launch (start us, length us, event | category | flops | bytes accessed | tf_op | source)
XLA Modules:
  0.0 319.0 jit_solution(1660180413172569511)
XLA Ops:
  3.6 78.0 %gather_shards.1 = (bf16[2,4,2,64,4224]{4,3,2,1,0:T(8,128)(2,1)}, bf16[2,4,2,128,1024]{4,3,2,1,0:T(8,128)(2,1)}, bf16[2,4,2,64,4096]{4,3,2,1,0:T(8,128)(2,1)}, bf16[2,4,2,128,1024]{4,3,2,1,0:T(8,128)(2,1)}) custom-call(bf16[1,1,1,64,4120]{4,3,2,1,0:T(8,128)(2,1)} %bitcast.161, bf16[1,1,1,128,1024]{4,3,2,1,0:T(8,128)(2,1)} %bitcast.164, ...), custom_call_target="tpu_custom_call" | custom-call | tf_op jit(solution)/shard_map/gather_shards/pallas_call | solution.py:653
  85.9 5.7 %fusion.35.p_ref = f32[2,112,4224]{2,1,0:T(8,128)S(1)} fusion(bf16[1024,4224,1]{1,0,2:T(8,128)(2,1)} %bitcast.138, bf16[2,112,1024]{2,1,0:T(8,128)(2,1)S(1)} %copy-done.14, f32[1024]{0:T(1024)S(1)} %mul.119, f32[2,112]{1,0:T(2,128)S(1)} %add_rsqrt_fusion.3), kind=kOutput, calls=%fused_computation.66 | convolution fusion | flops 1938685952 | bytes 12899200 | tf_op jit(solution)/shard_map/dot_general | solution.py:685
  91.8 4.6 %mix_forward.2 = bf16[2,112,2048]{2,1,0:T(8,128)(2,1)S(1)} custom-call(f32[2,112,4224]{2,1,0:T(8,128)S(1)} %fusion.35.p_ref, f32[2,112,128]{2,1,0:T(8,128)S(1)} %broadcast_in_dim.18.segc_ref, f32[2,8,112]{2,1,0:T(8,128)S(1)} %broadcast_in_dim.19.segr_ref, f32[8,1792]{1,0:T(8,128)S(1)} %pad.38.conv_ref, f32[8,128]{1,0:T(8,128)S(1)} %pad.39.head_ref, ...), custom_call_target="tpu_custom_call" | custom-call | tf_op jit(solution)/shard_map/mix_forward/pallas_call | solution.py:265
  97.6 5.7 %fusion.34 = f32[224,4096]{1,0:T(8,128)S(1)} fusion(bf16[1024,4096]{1,0:T(8,128)(2,1)} %bitcast.129, f32[224,1024]{1,0:T(8,128)S(1)} %get-tuple-element.99, f32[1024]{0:T(1024)S(1)} %mul.125, f32[224]{0:T(256)S(1)} %add_rsqrt_fusion.2), kind=kOutput, calls=%fused_computation.65 | convolution fusion | flops 1879736320 | bytes 12981120 | tf_op jit(solution)/shard_map/dot_general | solution.py:685
  104.6 4.8 %collective-permute-start = (bf16[224,1024]{1,0:T(8,128)(2,1)S(1)}, bf16[224,1024]{1,0:T(8,128)(2,1)S(1)}, u32[]{:S(2)}, u32[]{:S(2)}) collective-permute-start(bf16[224,1024]{1,0:T(8,128)(2,1)S(1)} %fusion.15), channel_id=1, source_target_pairs={{0,64},{1,65},{2,66},{3,67},{4,68},{5,69},{6,70},{7,71},{8,72},{9,... | collective-permute-start | bytes 1376264 | tf_op jit(solution)/shard_map/ppermute | solution.py:746
  109.5 9.7 %collective-permute-done = bf16[224,1024]{1,0:T(8,128)(2,1)S(1)} collective-permute-done((bf16[224,1024]{1,0:T(8,128)(2,1)S(1)}, bf16[224,1024]{1,0:T(8,128)(2,1)S(1)}, u32[]{:S(2)}, u32[]{:S(2)}) %collective-permute-start) | collective-permute-done | bytes 458784 | tf_op jit(solution)/shard_map/ppermute | solution.py:746
  119.7 6.3 %fusion.59.p_ref = f32[2,112,4224]{2,1,0:T(8,128)S(1)} fusion(bf16[2,112,1024]{2,1,0:T(8,128)(2,1)S(1)} %bitcast.153, bf16[1024,4224,1]{1,0,2:T(8,128)(2,1)} %bitcast.139), kind=kOutput, calls=%fused_computation.120 | convolution fusion | flops 1937768448 | bytes 12894208 | tf_op jit(solution)/shard_map/dot_general | solution.py:685
  126.0 4.7 %mix_forward.3 = (bf16[2,112,2048]{2,1,0:T(8,128)(2,1)S(1)}, f32[2,112,1536]{2,1,0:T(8,128)S(1)}) custom-call(f32[2,112,4224]{2,1,0:T(8,128)S(1)} %fusion.59.p_ref, f32[2,112,128]{2,1,0:T(8,128)S(1)} %broadcast_in_dim.18.segc_ref, f32[2,8,112]{2,1,0:T(8,128)S(1)} %broadcast_in_dim.19.segr_ref, f32[8,1792]{1,0:T(8,128)S(1)} %pad.38.conv_ref, ...), custom_call_target="tpu_custom_call" | custom-call | tf_op jit(solution)/shard_map/mix_forward/pallas_call | solution.py:265
  132.0 2.2 fusion.55
  136.4 2.8 multiply_reduce_fusion.2
  139.5 3.7 %fusion.60.gu_ref = f32[2,112,2048]{2,1,0:T(8,128)S(1)} fusion(bf16[2,112,1024]{2,1,0:T(8,128)(2,1)S(1)} %bitcast.158, bf16[2048,1024,1]{1,0,2:T(8,128)(2,1)} %bitcast.149), kind=kOutput, calls=%fused_computation.121 | convolution fusion | flops 939524096 | bytes 6488064 | tf_op jit(solution)/shard_map/dot_general | solution.py:689
  143.3 11.8 %mix_backward.2 = (bf16[2,112,4224]{2,1,0:T(8,128)(2,1)S(1)}, f32[2,8,1792]{2,1,0:T(8,128)}, f32[2,8,128]{2,1,0:T(8,128)}, f32[2,8,1536]{2,1,0:T(8,128)}) custom-call(f32[2,112,4224]{2,1,0:T(8,128)S(1)} %fusion.59.p_ref, f32[2,112,2048]{2,1,0:T(8,128)S(1)} %fusion.60.gu_ref, f32[2,112,1536]{2,1,0:T(8,128)S(1)} %get-tuple-element.32.y_ref, ...), custom_call_target="tpu_custom_call" | custom-call | tf_op jit(solution)/shard_map/mix_backward/pallas_call | solution.py:279
  155.2 2.8 fusion.22
  160.7 13.6 %collective-permute-done.1 = bf16[224,1024]{1,0:T(8,128)(2,1)} collective-permute-done((bf16[224,1024]{1,0:T(8,128)(2,1)}, bf16[224,1024]{1,0:T(8,128)(2,1)}, u32[]{:S(2)}, u32[]{:S(2)}) %collective-permute-start.1) | collective-permute-done | bytes 458784 | tf_op jit(solution)/shard_map/ppermute | solution.py:746
  175.5 5.3 %multiply_convert_fusion.1 = (bf16[224,2048]{1,0:T(8,128)(2,1)S(1)}, bf16[224,2048]{1,0:T(8,128)(2,1)S(1)}, bf16[224,2048]{1,0:T(8,128)(2,1)S(1)}) fusion(f32[224,4096]{1,0:T(8,128)} %copy-done.15, bf16[224,1024]{1,0:T(8,128)(2,1)S(1)} %broadcast_select_fusion, bf16[2048,1024]{1,0:T(8,128)(2,1)} %bitcast.178), kind=kOutput, calls=%fused_computation.13 | convolution fusion | flops 946405376 | bytes 11075584 | tf_op jit(solution)/shard_map/dot_general | solution.py:689
  182.8 3.3 %convolution_convert_fusion.2 = bf16[2048,1024]{1,0:T(8,128)(2,1)} fusion(bf16[224,2048]{1,0:T(8,128)(2,1)S(1)} %get-tuple-element.93, bf16[224,1024]{1,0:T(8,128)(2,1)S(1)} %broadcast_select_fusion), kind=kOutput, calls=%fused_computation.2 | convolution fusion | flops 941621248 | bytes 5570560 | tf_op jit(solution)/shard_map/dot_general | solution.py:695
  186.1 2.8 multiply_reduce_fusion
  188.9 5.7 %convolution_convert_fusion.1 = bf16[1024,4096]{1,0:T(8,128)(2,1)} fusion(bf16[224,2048]{1,0:T(8,128)(2,1)S(1)} %get-tuple-element.90, bf16[224,2048]{1,0:T(8,128)(2,1)S(1)} %get-tuple-element.89, f32[224,1024]{1,0:T(8,128)S(1)} %get-tuple-element.101, f32[224]{0:T(256)S(1)} %add_rsqrt_fusion, f32[1024]{0:T(1024)S(1)} %mul.125), kind=kOutput, calls=%fused_computation.1 | convolution fusion | flops 1887600640 | bytes 11146112 | tf_op jit(solution)/shard_map/dot_general | solution.py:695
  195.0 3.5 %convolution_convert_fusion.3 = bf16[2048,1024]{1,0:T(8,128)(2,1)} fusion(bf16[224,2048]{1,0:T(8,128)(2,1)S(1)} %bitcast.124, bf16[224,1024]{1,0:T(8,128)(2,1)S(1)} %fusion.57), kind=kOutput, calls=%fused_computation.3 | convolution fusion | flops 941621248 | bytes 5570560 | tf_op jit(solution)/shard_map/dot_general | solution.py:695
  200.8 11.0 %mix_backward.3 = (bf16[2,112,4224]{2,1,0:T(8,128)(2,1)S(1)}, f32[2,8,1792]{2,1,0:T(8,128)S(1)}, f32[2,8,128]{2,1,0:T(8,128)S(1)}, f32[2,8,1536]{2,1,0:T(8,128)S(1)}) custom-call(f32[2,112,4224]{2,1,0:T(8,128)S(1)} %copy-done.1, f32[2,112,2048]{2,1,0:T(8,128)S(1)} %fusion.61.gu_ref, f32[2,112,1536]{2,1,0:T(8,128)S(1)} %get-tuple-element.32.y_ref, ...), custom_call_target="tpu_custom_call" | custom-call | tf_op jit(solution)/shard_map/mix_backward/pallas_call | solution.py:279
  211.8 3.6 %fusion.31 = (bf16[1024]{0:T(1024)(128)(2,1)S(1)}, f32[224]{0:T(256)S(1)}, f32[224,1024]{1,0:T(8,128)}) fusion(bf16[224,1024]{1,0:T(8,128)(2,1)S(1)} %copy-done.7, f32[224]{0:T(256)S(1)} %add_rsqrt_fusion.1, f32[1024]{0:T(1024)S(1)} %mul.119, bf16[224,4224]{1,0:T(8,128)(2,1)S(1)} %bitcast.125, bf16[1024,4224]{1,0:T(8,128)(2,1)S(1)} %bitcast.145), kind=kOutput, calls=%fused_computation.52 | convolution fusion | flops 1939372800 | bytes 11927296 | tf_op jit(solution)/shard_map/dot_general | solution.py:689
  215.5 5.9 %convolution_convert_fusion = bf16[1024,4224]{1,0:T(8,128)(2,1)} fusion(bf16[224,1024]{1,0:T(8,128)(2,1)S(1)} %copy-done.11, bf16[224,4224]{1,0:T(8,128)(2,1)S(1)} %bitcast.126), kind=kOutput, calls=%fused_computation | convolution fusion | flops 1942093824 | bytes 11001856 | tf_op jit(solution)/shard_map/dot_general | solution.py:695
  222.8 86.0 %scatter_sums.1 = (bf16[64,4352]{1,0:T(8,128)(2,1)}, bf16[128,1024]{1,0:T(8,128)(2,1)}, bf16[64,4096]{1,0:T(8,128)(2,1)}, bf16[128,1024]{1,0:T(8,128)(2,1)}, f32...) custom-call(bf16[2,4,2,64,4224]{4,3,2,1,0:T(8,128)(2,1)} %bitcast.137, bf16[2,4,2,128,1024]{4,3,2,1,0:T(8,128)(2,1)} %bitcast.148, ...), custom_call_target="tpu_custom_call" | custom-call | tf_op jit(solution)/shard_map/scatter_sums/pallas_call | solution.py:548
  311.5 2.1 bitcast_convert_fusion.1
  (148 shorter events, 31.6 us)
Async XLA Ops:
  0.6 85.3 %copy-start.14 = (bf16[2,112,1024]{2,1,0:T(8,128)(2,1)S(1)}, bf16[2,112,1024]{2,1,0:T(8,128)(2,1)}, u32[]{:S(2)}) copy-start(bf16[2,112,1024]{2,1,0:T(8,128)(2,1)} %param.10) | copy-start | bytes 1376260
  104.6 14.6 %collective-permute-start = (bf16[224,1024]{1,0:T(8,128)(2,1)S(1)}, bf16[224,1024]{1,0:T(8,128)(2,1)S(1)}, u32[]{:S(2)}, u32[]{:S(2)}) collective-permute-start(bf16[224,1024]{1,0:T(8,128)(2,1)S(1)} %fusion.15), channel_id=1, source_target_pairs={{0,64},{1,65},{2,66},{3,67},{4,68},{5,69},{6,70},{7,71},{8,72},{9,... | collective-permute-start | bytes 1376264 | tf_op jit(solution)/shard_map/ppermute | solution.py:746
  119.4 11.3 %copy-start.5 = (bf16[224,1024]{1,0:T(8,128)(2,1)}, bf16[224,1024]{1,0:T(8,128)(2,1)S(1)}, u32[]{:S(2)}) copy-start(bf16[224,1024]{1,0:T(8,128)(2,1)S(1)} %get-tuple-element.88) | copy-start | bytes 1376260
  119.5 12.5 %slice-start = ((s8[8388608]{0:T(1024)(128)(4,1)}), s8[4194304]{0:T(1024)(128)(4,1)S(1)}, s32[]{:S(2)}) async-start(s8[8388608]{0:T(1024)(128)(4,1)} %bitcast.130), calls=%async_computation | async-start | bytes 8388608
  119.6 6.3 %copy-start.10 = (bf16[224,1024]{1,0:T(8,128)(2,1)}, bf16[224,1024]{1,0:T(8,128)(2,1)S(1)}, u32[]{:S(2)}) copy-start(bf16[224,1024]{1,0:T(8,128)(2,1)S(1)} %fusion.21) | copy-start | bytes 1376260
  119.7 11.1 %copy-start.3 = (bf16[2,4,2,128,1024]{4,3,2,1,0:T(8,128)(2,1)S(1)}, bf16[2,4,2,128,1024]{4,3,2,1,0:T(8,128)(2,1)}, u32[]{:S(2)}) copy-start(bf16[2,4,2,128,1024]{4,3,2,1,0:T(8,128)(2,1)} %get-tuple-element.28) | copy-start | bytes 12582916
  119.7 12.3 %slice-start.1 = ((s8[8388608]{0:T(1024)(128)(4,1)}), s8[4194304]{0:T(1024)(128)(4,1)S(1)}, s32[]{:S(2)}) async-start(s8[8388608]{0:T(1024)(128)(4,1)} %bitcast.130), calls=%async_computation.1 | async-start | bytes 8388608
  126.0 17.3 %copy-start = (f32[2,112,4224]{2,1,0:T(8,128)}, f32[2,112,4224]{2,1,0:T(8,128)S(1)}, u32[]{:S(2)}) copy-start(f32[2,112,4224]{2,1,0:T(8,128)S(1)} %fusion.59.p_ref) | copy-start | bytes 11354116
  136.4 18.7 %slice-start.4 = ((s8[8650752]{0:T(1024)(128)(4,1)}), s8[4194304]{0:T(1024)(128)(4,1)S(1)}, s32[]{:S(2)}) async-start(s8[8650752]{0:T(1024)(128)(4,1)} %bitcast.140), calls=%async_computation.4 | async-start | bytes 8388608
  136.4 18.7 %slice-start.5 = ((s8[8650752]{0:T(1024)(128)(4,1)}), s8[262144]{0:T(1024)(128)(4,1)S(1)}, s32[]{:S(2)}) async-start(s8[8650752]{0:T(1024)(128)(4,1)} %bitcast.140), calls=%async_computation.5 | async-start | bytes 524288
  139.5 15.6 %slice-start.6 = ((s8[8650752]{0:T(1024)(128)(4,1)}), s8[4194304]{0:T(1024)(128)(4,1)S(1)}, s32[]{:S(2)}) async-start(s8[8650752]{0:T(1024)(128)(4,1)} %bitcast.140), calls=%async_computation.6 | async-start | bytes 8388608
  143.3 11.9 %copy-start.6 = (bf16[224,1024]{1,0:T(8,128)(2,1)S(1)}, bf16[224,1024]{1,0:T(8,128)(2,1)}, u32[]{:S(2)}) copy-start(bf16[224,1024]{1,0:T(8,128)(2,1)} %copy-done.5) | copy-start | bytes 1376260
  159.3 15.0 %collective-permute-start.1 = (bf16[224,1024]{1,0:T(8,128)(2,1)}, bf16[224,1024]{1,0:T(8,128)(2,1)}, u32[]{:S(2)}, u32[]{:S(2)}) collective-permute-start(bf16[224,1024]{1,0:T(8,128)(2,1)} %fusion.26), channel_id=1, source_target_pairs={{64,0},{65,1},{66,2},{67,3},{68,4},{69,5},{70,6},{71,7},{72,8},{73... | collective-permute-start | bytes 1376264 | tf_op jit(solution)/shard_map/ppermute | solution.py:746
  175.5 19.2 %copy-start.8 = (bf16[224,1024]{1,0:T(8,128)(2,1)}, bf16[224,1024]{1,0:T(8,128)(2,1)S(1)}, u32[]{:S(2)}) copy-start(bf16[224,1024]{1,0:T(8,128)(2,1)S(1)} %broadcast_select_fusion) | copy-start | bytes 1376260
  188.9 5.7 %copy-start.18 = (f32[224,1024]{1,0:T(8,128)}, f32[224,1024]{1,0:T(8,128)S(1)}, u32[]{:S(2)}) copy-start(f32[224,1024]{1,0:T(8,128)S(1)} %get-tuple-element.106) | copy-start | bytes 2752516
  188.9 22.8 %slice-start.7 = ((s8[8650752]{0:T(1024)(128)(4,1)}), s8[4194304]{0:T(1024)(128)(4,1)S(1)}, s32[]{:S(2)}) async-start(s8[8650752]{0:T(1024)(128)(4,1)} %bitcast.143), calls=%async_computation.7 | async-start | bytes 8388608
  194.7 17.1 %slice-start.8 = ((s8[8650752]{0:T(1024)(128)(4,1)}), s8[4194304]{0:T(1024)(128)(4,1)S(1)}, s32[]{:S(2)}) async-start(s8[8650752]{0:T(1024)(128)(4,1)} %bitcast.143), calls=%async_computation.8 | async-start | bytes 8388608
  198.4 13.3 %slice-start.9 = ((s8[8650752]{0:T(1024)(128)(4,1)}), s8[262144]{0:T(1024)(128)(4,1)S(1)}, s32[]{:S(2)}) async-start(s8[8650752]{0:T(1024)(128)(4,1)} %bitcast.143), calls=%async_computation.9 | async-start | bytes 524288
  200.8 11.0 %copy-start.7 = (bf16[224,1024]{1,0:T(8,128)(2,1)S(1)}, bf16[224,1024]{1,0:T(8,128)(2,1)}, u32[]{:S(2)}) copy-start(bf16[224,1024]{1,0:T(8,128)(2,1)} %copy-done.5) | copy-start | bytes 1376260
  222.8 92.9 %copy-start.9 = (bf16[224,1024]{1,0:T(8,128)(2,1)S(1)}, bf16[224,1024]{1,0:T(8,128)(2,1)}, u32[]{:S(2)}) copy-start(bf16[224,1024]{1,0:T(8,128)(2,1)} %copy-done.8) | copy-start | bytes 1376260
  308.8 6.9 %copy-start.19 = (f32[224,1024]{1,0:T(8,128)S(1)}, f32[224,1024]{1,0:T(8,128)}, u32[]{:S(2)}) copy-start(f32[224,1024]{1,0:T(8,128)} %copy-done.18) | copy-start | bytes 2752516
  308.8 6.9 %copy-start.20 = (f32[224,1024]{1,0:T(8,128)S(1)}, f32[224,1024]{1,0:T(8,128)}, u32[]{:S(2)}) copy-start(f32[224,1024]{1,0:T(8,128)} %get-tuple-element.107) | copy-start | bytes 2752516
  311.5 5.7 %copy-start.21 = (bf16[128,1024]{1,0:T(8,128)(2,1)S(1)}, bf16[128,1024]{1,0:T(8,128)(2,1)}, u32[]{:S(2)}) copy-start(bf16[128,1024]{1,0:T(8,128)(2,1)} %get-tuple-element.42) | copy-start | bytes 786436
  311.5 5.7 %copy-start.22 = (bf16[128,1024]{1,0:T(8,128)(2,1)S(1)}, bf16[128,1024]{1,0:T(8,128)(2,1)}, u32[]{:S(2)}) copy-start(bf16[128,1024]{1,0:T(8,128)(2,1)} %get-tuple-element.44) | copy-start | bytes 786436
  (15 other events, 54.8 us)
